TPU v7x, 512 devices: a whole 4x8x8 slice. The times are simulated.
512 devices in a mesh: band: 32 (over x, y), lev: 16 (over z, core).
Axes of the slice: x: 4, y: 8, z: 8, core: 2. Of those that a mesh axis runs over, the one named last changes fastest.
Arguments:
- increment: bfloat16 [2, 128, 1024, 128], P(None, 'lev', 'band'), may hold values from -6 to 6
- diffusivity: bfloat16 [2, 128, 1024, 128], P(None, 'lev', 'band'), may hold values from 0.049804688 to 0.15917969
- sigma: bfloat16 [2, 128, 1024, 128], P(None, 'lev', 'band'), may hold values from 0.5 to 2
- jacobian: bfloat16 [4, 256, 2, 128], P(None, None, None, 'lev'), may hold values from -0.375 to 0.375
- rinv: float32 [256], replicated, may hold values from 0.25 to 4
- innovation: bfloat16 [32, 256, 32, 128], P('band'), may hold values from -6 to 6
- obs_column: int32 [32, 32, 128], P('band'), may hold values from 0 to 4095
- obs_table: int32 [32, 32, 128], P('band'), may hold values from 0 to 3
- obs_count: int32 [32, 32], P('band'), may hold values from 0 to 128, as said below
Outputs:
- gradient: float32 [2, 128, 1024, 128], P(None, 'lev', 'band')
Inputs may be any that keep to these rules, and one draw needn't show every extreme that they name: The profiles that owner o takes from band s fill its first obs_count[o, s] slots of that band; the most, 128, is reached by every owner from some band and by one owner from every band.
All inputs are finite; a program needn't handle non-finite values.
Results may differ from a plain program's by a relative error of at most 0.006.
Values may be sent and summed in bfloat16 or wider, within the bound.
A program may use at most 64 MiB of HBM per device.

v0:
```python
import jax
import jax.numpy as jnp
from jax import lax
from jax.sharding import PartitionSpec as P

NTAB = 4
STEPS = 3


def padded_2(value, sides, width, wrap):
    for axis, dim in sides:
        count, length = (lax.axis_size(axis), value.shape[dim])
        up = [(i, (i + 1) % count) for i in range(count if wrap else count - 1)]
        down = [(j, i) for i, j in up]
        last = lax.slice_in_dim(value, length - width, length, axis=dim)
        leading = lax.slice_in_dim(value, 0, width, axis=dim)
        before = lax.ppermute(last, axis, up)
        after = lax.ppermute(leading, axis, down)
        value = jnp.concatenate([before, value, after], axis=dim)
    return value


def lap_ext(field):
    padded = jnp.pad(field, ((0, 0), (1, 1), (1, 1), (1, 1)))
    total = padded[:, 2:, 1:-1, 1:-1] + padded[:, :-2, 1:-1, 1:-1]
    total = total + padded[:, 1:-1, 2:, 1:-1] + padded[:, 1:-1, :-2, 1:-1]
    total = total + padded[:, 1:-1, 1:-1, 2:] + padded[:, 1:-1, 1:-1, :-2]
    return total - 6.0 * field


def extend(stacked, margin):
    wider = padded_2(stacked, (("band", 3),), margin, True)
    return padded_2(wider, (("lev", 2),), margin, False)


def inner(field, margin):
    return field[:, margin:-margin, margin:-margin, :]


def body(
    increment, diffusivity, sigma, jacobian, rinv, innovation, obs_column, obs_table, obs_count
):
    coeff = diffusivity.astype(jnp.float32)
    scale = sigma.astype(jnp.float32)
    fields, levels, longs, lats = increment.shape
    width = fields * levels
    field = increment.astype(jnp.float32)
    coeff_pad = jnp.pad(coeff, ((0, 0), (1, 1), (1, 1), (0, 0)))
    for step in range(STEPS):
        spread = extend(field[None], 1)[0]
        field = inner(spread + coeff_pad * lap_ext(spread), 1)
    state = (scale * field).astype(jnp.bfloat16)
    owners, slots = (obs_column.shape[1], obs_column.shape[2])
    col_index = obs_column[0].reshape(-1)
    profile = jnp.take(state.reshape(width, longs * lats), col_index, axis=1).reshape(
        width, owners, slots
    )
    arrived = lax.all_to_all(profile, "band", split_axis=1, concat_axis=1, tiled=True).reshape(
        width, -1
    )
    tables = obs_table[0].reshape(-1)
    weights = jacobian.reshape(NTAB, jacobian.shape[1], width)
    channels = weights.shape[1]
    partial_value = jnp.zeros((channels, arrived.shape[1]), jnp.float32)
    for table in range(NTAB):
        product = jnp.dot(weights[table], arrived, preferred_element_type=jnp.float32)
        partial_value = partial_value + jnp.where(tables[None, :] == table, product, 0.0)
    slot_ids = jnp.arange(slots, dtype=jnp.int32)
    valid = (slot_ids[None, :] < obs_count[0][:, None]).reshape(-1)
    observed = innovation[0].reshape(channels, -1)
    evolved = lax.psum(partial_value.astype(jnp.bfloat16), "lev").astype(jnp.float32)
    resid = jnp.where(
        valid[None, :], rinv[:, None] * (evolved - observed.astype(jnp.float32)), 0.0
    ).astype(jnp.bfloat16)
    back = jnp.zeros((width, arrived.shape[1]), jnp.float32)
    for table in range(NTAB):
        masked = jnp.where(tables[None, :] == table, resid, jnp.zeros_like(resid))
        back = back + jnp.dot(weights[table].T, masked, preferred_element_type=jnp.float32)
    returned = back.astype(jnp.bfloat16).reshape(width, owners, slots)
    home = lax.all_to_all(returned, "band", split_axis=1, concat_axis=1, tiled=True).reshape(
        width, -1
    )
    adjoint = (
        jnp.zeros((width, longs * lats), jnp.float32).at[:, col_index].add(home.astype(jnp.float32))
    )
    field = scale * adjoint.reshape(fields, levels, longs, lats)
    for step in range(STEPS):
        spread = extend((coeff * field)[None], 1)[0]
        field = field + inner(lap_ext(spread), 1)
    return increment.astype(jnp.float32) + field


def solution(mesh):
    in_specs = (
        P(None, "lev", "band", None),
        P(None, "lev", "band", None),
        P(None, "lev", "band", None),
        P(None, None, None, "lev"),
        P(),
        P("band", None, None, None),
        P("band", None, None),
        P("band", None, None),
        P("band", None),
    )
    out_specs = P(None, "lev", "band", None)
    return jax.shard_map(body, mesh=mesh, in_specs=in_specs, out_specs=out_specs, check_vma=False)
```

profile of v0, /device:TPU:1, one launch (start us, length us, event | category | flops | bytes accessed | tf_op | source)
XLA Modules:
  0.0 338.6 jit_solution(9852963366047569145)
XLA Ops:
  7.5 4.0 %collective-permute-start = (f32[1,2,8,1,128]{4,3,2,1,0:T(1,128)S(1)}, f32[1,2,8,1,128]{4,3,2,1,0:T(1,128)S(1)}, u32[]{:S(2)}, u32[]{:S(2)}) collective-permute-start(f32[1,2,8,1,128]{4,3,2,1,0:T(1,128)S(1)} %get-tuple-element.61), channel_id=1, source_target_pairs={{0,16},{16,32},{32,48},{48,64},{64,80},{80,96},{96,112},{112,128},... | collective-permute-start | bytes 24584 | tf_op jit(solution)/shard_map/ppermute | solution.py:17
  11.5 6.0 %collective-permute-start.1 = (f32[1,2,8,1,128]{4,3,2,1,0:T(1,128)S(1)}, f32[1,2,8,1,128]{4,3,2,1,0:T(1,128)S(1)}, u32[]{:S(2)}, u32[]{:S(2)}) collective-permute-start(f32[1,2,8,1,128]{4,3,2,1,0:T(1,128)S(1)} %get-tuple-element.62), channel_id=1, source_target_pairs={{16,0},{32,16},{48,32},{64,48},{80,64},{96,80},{112,96},{128,112},... | collective-permute-start | bytes 24584 | tf_op jit(solution)/shard_map/ppermute | solution.py:18
  18.3 5.4 %collective-permute-start.2 = (f32[1,2,1,34,128]{4,3,2,1,0:T(8,128)S(1)}, f32[1,2,1,34,128]{4,3,2,1,0:T(8,128)S(1)}, u32[]{:S(2)}, u32[]{:S(2)}) collective-permute-start(f32[1,2,1,34,128]{4,3,2,1,0:T(8,128)S(1)} %get-tuple-element.49), channel_id=1, source_target_pairs={{0,1},{1,2},{2,3},{3,4},{4,5},{5,6},{6,7},{7,8},{8,9},{9,10},{10,1... | collective-permute-start | bytes 104456 | tf_op jit(solution)/shard_map/ppermute | solution.py:17
  23.8 4.4 %collective-permute-start.3 = (f32[1,2,1,34,128]{4,3,2,1,0:T(8,128)S(1)}, f32[1,2,1,34,128]{4,3,2,1,0:T(8,128)S(1)}, u32[]{:S(2)}, u32[]{:S(2)}) collective-permute-start(f32[1,2,1,34,128]{4,3,2,1,0:T(8,128)S(1)} %get-tuple-element.50), channel_id=1, source_target_pairs={{1,0},{2,1},{3,2},{4,3},{5,4},{6,5},{7,6},{8,7},{9,8},{10,9},{11,1... | collective-permute-start | bytes 104456 | tf_op jit(solution)/shard_map/ppermute | solution.py:18
  31.6 7.2 %collective-permute-start.5 = (f32[1,2,8,1,128]{4,3,2,1,0:T(1,128)S(1)}, f32[1,2,8,1,128]{4,3,2,1,0:T(1,128)S(1)}, u32[]{:S(2)}, u32[]{:S(2)}) collective-permute-start(f32[1,2,8,1,128]{4,3,2,1,0:T(1,128)S(1)} %get-tuple-element.60), channel_id=1, source_target_pairs={{16,0},{32,16},{48,32},{64,48},{80,64},{96,80},{112,96},{128,112},... | collective-permute-start | bytes 24584 | tf_op jit(solution)/shard_map/ppermute | solution.py:18
  44.3 3.3 collective-permute-done.7
  50.3 7.2 %collective-permute-start.9 = (f32[1,2,8,1,128]{4,3,2,1,0:T(1,128)S(1)}, f32[1,2,8,1,128]{4,3,2,1,0:T(1,128)S(1)}, u32[]{:S(2)}, u32[]{:S(2)}) collective-permute-start(f32[1,2,8,1,128]{4,3,2,1,0:T(1,128)S(1)} %get-tuple-element.58), channel_id=1, source_target_pairs={{16,0},{32,16},{48,32},{64,48},{80,64},{96,80},{112,96},{128,112},... | collective-permute-start | bytes 24584 | tf_op jit(solution)/shard_map/ppermute | solution.py:18
  63.1 3.4 collective-permute-done.11
  67.6 12.1 %gather_fusion = bf16[4096,16]{1,0:T(8,128)(2,1)S(1)} fusion(bf16[16,4096]{0,1:T(8,128)(2,1)S(1)} %copy.23, s32[4096]{0:T(1024)S(1)} %broadcast_clamp_fusion), kind=kCustom, calls=%fused_computation | custom fusion | bytes 278528 | tf_op jit(solution)/shard_map/jit(_take)/gather | solution.py:55
  80.7 7.0 %all-to-all-start = ((bf16[16,32,128]{2,0,1:T(8,128)(2,1)}), bf16[16,32,128]{2,0,1:T(8,128)(2,1)S(1)}, u32[]{:S(2)}, u32[]{:S(2)}) async-start(bf16[16,32,128]{2,0,1:T(8,128)(2,1)} %broadcast_select_fusion), calls=%async_computation | async-start | bytes 262144 | tf_op jit(solution)/shard_map/all_to_all | solution.py:58
  87.8 9.0 %all-to-all-done = bf16[16,32,128]{2,0,1:T(8,128)(2,1)S(1)} async-done(((bf16[16,32,128]{2,0,1:T(8,128)(2,1)}), bf16[16,32,128]{2,0,1:T(8,128)(2,1)S(1)}, u32[]{:S(2)}, u32[]{:S(2)}) %all-to-all-start) | async-done | bytes 131104 | tf_op jit(solution)/shard_map/all_to_all | solution.py:58
  103.6 3.2 copy.26
  106.8 116.9 %all-reduce.9.cloned.1.call-done = bf16[256,4096]{0,1:T(8,128)(2,1)} async-done(((bf16[256,4096]{0,1:T(8,128)(2,1)}), bf16[256,4096]{0,1:T(8,128)(2,1)}) %all-reduce.9.cloned.1.call-update) | async-done | bytes 2097168 | tf_op jit(solution)/shard_map/psum | solution.py:71
  223.8 3.2 fusion.8
  230.1 18.2 %all_to_all.10 = bf16[16,32,128]{2,0,1:T(8,128)(2,1)S(1)} all-to-all(bf16[16,32,128]{2,0,1:T(8,128)(2,1)S(1)} %bitcast.128), channel_id=1, replica_groups=mesh['band'=32,'lev'=16] {'band'}, dimensions={1} | all-to-all | bytes 262144 | tf_op jit(solution)/shard_map/all_to_all | solution.py:80
  250.3 23.2 %scatter_custom_fusion = f32[16,4096]{0,1:T(8,128)S(1)} fusion(s32[4096]{0:T(1024)S(1)} %bitcast.131, f32[4096,16]{1,0:T(8,128)} %copy.29, f32[]{:T(128)} %constant.10.clone.1), kind=kCustom, calls=%fused_computation.69 | custom fusion | flops 65536 | bytes 262656 | tf_op jit(solution)/shard_map/scatter-add | solution.py:84
  274.2 2.8 collective-permute-start.12
  277.0 5.8 %collective-permute-start.13 = (f32[1,2,8,1,128]{4,3,2,1,0:T(1,128)S(1)}, f32[1,2,8,1,128]{4,3,2,1,0:T(1,128)S(1)}, u32[]{:S(2)}, u32[]{:S(2)}) collective-permute-start(f32[1,2,8,1,128]{4,3,2,1,0:T(1,128)S(1)} %get-tuple-element.56), channel_id=1, source_target_pairs={{16,0},{32,16},{48,32},{64,48},{80,64},{96,80},{112,96},{128,112},... | collective-permute-start | bytes 24584 | tf_op jit(solution)/shard_map/ppermute | solution.py:18
  283.6 4.0 %collective-permute-start.14 = (f32[1,2,1,34,128]{4,3,2,1,0:T(8,128)S(1)}, f32[1,2,1,34,128]{4,3,2,1,0:T(8,128)S(1)}, u32[]{:S(2)}, u32[]{:S(2)}) collective-permute-start(f32[1,2,1,34,128]{4,3,2,1,0:T(8,128)S(1)} %get-tuple-element.43), channel_id=1, source_target_pairs={{0,1},{1,2},{2,3},{3,4},{4,5},{5,6},{6,7},{7,8},{8,9},{9,10},{10,1... | collective-permute-start | bytes 104456 | tf_op jit(solution)/shard_map/ppermute | solution.py:17
  287.6 2.8 collective-permute-start.15
  295.5 7.2 %collective-permute-start.17 = (f32[1,2,8,1,128]{4,3,2,1,0:T(1,128)S(1)}, f32[1,2,8,1,128]{4,3,2,1,0:T(1,128)S(1)}, u32[]{:S(2)}, u32[]{:S(2)}) collective-permute-start(f32[1,2,8,1,128]{4,3,2,1,0:T(1,128)S(1)} %get-tuple-element.54), channel_id=1, source_target_pairs={{16,0},{32,16},{48,32},{64,48},{80,64},{96,80},{112,96},{128,112},... | collective-permute-start | bytes 24584 | tf_op jit(solution)/shard_map/ppermute | solution.py:18
  308.3 3.4 collective-permute-done.19
  314.3 7.2 %collective-permute-start.21 = (f32[1,2,8,1,128]{4,3,2,1,0:T(1,128)S(1)}, f32[1,2,8,1,128]{4,3,2,1,0:T(1,128)S(1)}, u32[]{:S(2)}, u32[]{:S(2)}) collective-permute-start(f32[1,2,8,1,128]{4,3,2,1,0:T(1,128)S(1)} %get-tuple-element.52), channel_id=1, source_target_pairs={{16,0},{32,16},{48,32},{64,48},{80,64},{96,80},{112,96},{128,112},... | collective-permute-start | bytes 24584 | tf_op jit(solution)/shard_map/ppermute | solution.py:18
  327.1 3.4 collective-permute-done.23
  (106 shorter events, 54.1 us)
Async XLA Ops:
  7.5 10.1 %collective-permute-start = (f32[1,2,8,1,128]{4,3,2,1,0:T(1,128)S(1)}, f32[1,2,8,1,128]{4,3,2,1,0:T(1,128)S(1)}, u32[]{:S(2)}, u32[]{:S(2)}) collective-permute-start(f32[1,2,8,1,128]{4,3,2,1,0:T(1,128)S(1)} %get-tuple-element.61), channel_id=1, source_target_pairs={{0,16},{16,32},{32,48},{48,64},{64,80},{80,96},{96,112},{112,128},... | collective-permute-start | bytes 24584 | tf_op jit(solution)/shard_map/ppermute | solution.py:17
  11.5 6.8 %collective-permute-start.1 = (f32[1,2,8,1,128]{4,3,2,1,0:T(1,128)S(1)}, f32[1,2,8,1,128]{4,3,2,1,0:T(1,128)S(1)}, u32[]{:S(2)}, u32[]{:S(2)}) collective-permute-start(f32[1,2,8,1,128]{4,3,2,1,0:T(1,128)S(1)} %get-tuple-element.62), channel_id=1, source_target_pairs={{16,0},{32,16},{48,32},{64,48},{80,64},{96,80},{112,96},{128,112},... | collective-permute-start | bytes 24584 | tf_op jit(solution)/shard_map/ppermute | solution.py:18
  18.3 10.7 %collective-permute-start.2 = (f32[1,2,1,34,128]{4,3,2,1,0:T(8,128)S(1)}, f32[1,2,1,34,128]{4,3,2,1,0:T(8,128)S(1)}, u32[]{:S(2)}, u32[]{:S(2)}) collective-permute-start(f32[1,2,1,34,128]{4,3,2,1,0:T(8,128)S(1)} %get-tuple-element.49), channel_id=1, source_target_pairs={{0,1},{1,2},{2,3},{3,4},{4,5},{5,6},{6,7},{7,8},{8,9},{9,10},{10,1... | collective-permute-start | bytes 104456 | tf_op jit(solution)/shard_map/ppermute | solution.py:17
  23.8 5.3 %collective-permute-start.3 = (f32[1,2,1,34,128]{4,3,2,1,0:T(8,128)S(1)}, f32[1,2,1,34,128]{4,3,2,1,0:T(8,128)S(1)}, u32[]{:S(2)}, u32[]{:S(2)}) collective-permute-start(f32[1,2,1,34,128]{4,3,2,1,0:T(8,128)S(1)} %get-tuple-element.50), channel_id=1, source_target_pairs={{1,0},{2,1},{3,2},{4,3},{5,4},{6,5},{7,6},{8,7},{9,8},{10,9},{11,1... | collective-permute-start | bytes 104456 | tf_op jit(solution)/shard_map/ppermute | solution.py:18
  29.6 9.2 %collective-permute-start.4 = (f32[1,2,8,1,128]{4,3,2,1,0:T(1,128)S(1)}, f32[1,2,8,1,128]{4,3,2,1,0:T(1,128)S(1)}, u32[]{:S(2)}, u32[]{:S(2)}) collective-permute-start(f32[1,2,8,1,128]{4,3,2,1,0:T(1,128)S(1)} %get-tuple-element.59), channel_id=1, source_target_pairs={{0,16},{16,32},{32,48},{48,64},{64,80},{80,96},{96,112},{112,128},... | collective-permute-start | bytes 24584 | tf_op jit(solution)/shard_map/ppermute | solution.py:17
  31.6 8.0 %collective-permute-start.5 = (f32[1,2,8,1,128]{4,3,2,1,0:T(1,128)S(1)}, f32[1,2,8,1,128]{4,3,2,1,0:T(1,128)S(1)}, u32[]{:S(2)}, u32[]{:S(2)}) collective-permute-start(f32[1,2,8,1,128]{4,3,2,1,0:T(1,128)S(1)} %get-tuple-element.60), channel_id=1, source_target_pairs={{16,0},{32,16},{48,32},{64,48},{80,64},{96,80},{112,96},{128,112},... | collective-permute-start | bytes 24584 | tf_op jit(solution)/shard_map/ppermute | solution.py:18
  39.6 4.7 %collective-permute-start.6 = (f32[1,2,1,34,128]{4,3,2,1,0:T(8,128)S(1)}, f32[1,2,1,34,128]{4,3,2,1,0:T(8,128)S(1)}, u32[]{:S(2)}, u32[]{:S(2)}) collective-permute-start(f32[1,2,1,34,128]{4,3,2,1,0:T(8,128)S(1)} %get-tuple-element.47), channel_id=1, source_target_pairs={{0,1},{1,2},{2,3},{3,4},{4,5},{5,6},{6,7},{7,8},{8,9},{9,10},{10,1... | collective-permute-start | bytes 104456 | tf_op jit(solution)/shard_map/ppermute | solution.py:17
  42.4 5.3 %collective-permute-start.7 = (f32[1,2,1,34,128]{4,3,2,1,0:T(8,128)S(1)}, f32[1,2,1,34,128]{4,3,2,1,0:T(8,128)S(1)}, u32[]{:S(2)}, u32[]{:S(2)}) collective-permute-start(f32[1,2,1,34,128]{4,3,2,1,0:T(8,128)S(1)} %get-tuple-element.48), channel_id=1, source_target_pairs={{1,0},{2,1},{3,2},{4,3},{5,4},{6,5},{7,6},{8,7},{9,8},{10,9},{11,1... | collective-permute-start | bytes 104456 | tf_op jit(solution)/shard_map/ppermute | solution.py:18
  48.2 9.3 %collective-permute-start.8 = (f32[1,2,8,1,128]{4,3,2,1,0:T(1,128)S(1)}, f32[1,2,8,1,128]{4,3,2,1,0:T(1,128)S(1)}, u32[]{:S(2)}, u32[]{:S(2)}) collective-permute-start(f32[1,2,8,1,128]{4,3,2,1,0:T(1,128)S(1)} %get-tuple-element.57), channel_id=1, source_target_pairs={{0,16},{16,32},{32,48},{48,64},{64,80},{80,96},{96,112},{112,128},... | collective-permute-start | bytes 24584 | tf_op jit(solution)/shard_map/ppermute | solution.py:17
  50.3 8.0 %collective-permute-start.9 = (f32[1,2,8,1,128]{4,3,2,1,0:T(1,128)S(1)}, f32[1,2,8,1,128]{4,3,2,1,0:T(1,128)S(1)}, u32[]{:S(2)}, u32[]{:S(2)}) collective-permute-start(f32[1,2,8,1,128]{4,3,2,1,0:T(1,128)S(1)} %get-tuple-element.58), channel_id=1, source_target_pairs={{16,0},{32,16},{48,32},{64,48},{80,64},{96,80},{112,96},{128,112},... | collective-permute-start | bytes 24584 | tf_op jit(solution)/shard_map/ppermute | solution.py:18
  58.3 4.7 %collective-permute-start.10 = (f32[1,2,1,34,128]{4,3,2,1,0:T(8,128)S(1)}, f32[1,2,1,34,128]{4,3,2,1,0:T(8,128)S(1)}, u32[]{:S(2)}, u32[]{:S(2)}) collective-permute-start(f32[1,2,1,34,128]{4,3,2,1,0:T(8,128)S(1)} %get-tuple-element.45), channel_id=1, source_target_pairs={{0,1},{1,2},{2,3},{3,4},{4,5},{5,6},{6,7},{7,8},{8,9},{9,10},{10,1... | collective-permute-start | bytes 104456 | tf_op jit(solution)/shard_map/ppermute | solution.py:17
  61.1 5.3 %collective-permute-start.11 = (f32[1,2,1,34,128]{4,3,2,1,0:T(8,128)S(1)}, f32[1,2,1,34,128]{4,3,2,1,0:T(8,128)S(1)}, u32[]{:S(2)}, u32[]{:S(2)}) collective-permute-start(f32[1,2,1,34,128]{4,3,2,1,0:T(8,128)S(1)} %get-tuple-element.46), channel_id=1, source_target_pairs={{1,0},{2,1},{3,2},{4,3},{5,4},{6,5},{7,6},{8,7},{9,8},{10,9},{11,1... | collective-permute-start | bytes 104456 | tf_op jit(solution)/shard_map/ppermute | solution.py:18
  80.7 16.1 %all-to-all-start = ((bf16[16,32,128]{2,0,1:T(8,128)(2,1)}), bf16[16,32,128]{2,0,1:T(8,128)(2,1)S(1)}, u32[]{:S(2)}, u32[]{:S(2)}) async-start(bf16[16,32,128]{2,0,1:T(8,128)(2,1)} %broadcast_select_fusion), calls=%async_computation | async-start | bytes 262144 | tf_op jit(solution)/shard_map/all_to_all | solution.py:58
  87.7 136.0 %all-reduce.9.cloned.1.call-start = ((), (), s32[]{:S(2)}) async-start(), calls=%async_computation.2 | async-start | bytes 4194304 | tf_op jit(solution)/shard_map/psum | solution.py:71
  274.2 8.6 %collective-permute-start.12 = (f32[1,2,8,1,128]{4,3,2,1,0:T(1,128)S(1)}, f32[1,2,8,1,128]{4,3,2,1,0:T(1,128)S(1)}, u32[]{:S(2)}, u32[]{:S(2)}) collective-permute-start(f32[1,2,8,1,128]{4,3,2,1,0:T(1,128)S(1)} %get-tuple-element.55), channel_id=1, source_target_pairs={{0,16},{16,32},{32,48},{48,64},{64,80},{80,96},{96,112},{112,128},... | collective-permute-start | bytes 24584 | tf_op jit(solution)/shard_map/ppermute | solution.py:17
  277.0 6.6 %collective-permute-start.13 = (f32[1,2,8,1,128]{4,3,2,1,0:T(1,128)S(1)}, f32[1,2,8,1,128]{4,3,2,1,0:T(1,128)S(1)}, u32[]{:S(2)}, u32[]{:S(2)}) collective-permute-start(f32[1,2,8,1,128]{4,3,2,1,0:T(1,128)S(1)} %get-tuple-element.56), channel_id=1, source_target_pairs={{16,0},{32,16},{48,32},{64,48},{80,64},{96,80},{112,96},{128,112},... | collective-permute-start | bytes 24584 | tf_op jit(solution)/shard_map/ppermute | solution.py:18
  283.6 6.8 %collective-permute-start.14 = (f32[1,2,1,34,128]{4,3,2,1,0:T(8,128)S(1)}, f32[1,2,1,34,128]{4,3,2,1,0:T(8,128)S(1)}, u32[]{:S(2)}, u32[]{:S(2)}) collective-permute-start(f32[1,2,1,34,128]{4,3,2,1,0:T(8,128)S(1)} %get-tuple-element.43), channel_id=1, source_target_pairs={{0,1},{1,2},{2,3},{3,4},{4,5},{5,6},{6,7},{7,8},{8,9},{9,10},{10,1... | collective-permute-start | bytes 104456 | tf_op jit(solution)/shard_map/ppermute | solution.py:17
  287.6 5.3 %collective-permute-start.15 = (f32[1,2,1,34,128]{4,3,2,1,0:T(8,128)S(1)}, f32[1,2,1,34,128]{4,3,2,1,0:T(8,128)S(1)}, u32[]{:S(2)}, u32[]{:S(2)}) collective-permute-start(f32[1,2,1,34,128]{4,3,2,1,0:T(8,128)S(1)} %get-tuple-element.44), channel_id=1, source_target_pairs={{1,0},{2,1},{3,2},{4,3},{5,4},{6,5},{7,6},{8,7},{9,8},{10,9},{11,1... | collective-permute-start | bytes 104456 | tf_op jit(solution)/shard_map/ppermute | solution.py:18
  293.6 9.2 %collective-permute-start.16 = (f32[1,2,8,1,128]{4,3,2,1,0:T(1,128)S(1)}, f32[1,2,8,1,128]{4,3,2,1,0:T(1,128)S(1)}, u32[]{:S(2)}, u32[]{:S(2)}) collective-permute-start(f32[1,2,8,1,128]{4,3,2,1,0:T(1,128)S(1)} %get-tuple-element.53), channel_id=1, source_target_pairs={{0,16},{16,32},{32,48},{48,64},{64,80},{80,96},{96,112},{112,128},... | collective-permute-start | bytes 24584 | tf_op jit(solution)/shard_map/ppermute | solution.py:17
  295.5 8.0 %collective-permute-start.17 = (f32[1,2,8,1,128]{4,3,2,1,0:T(1,128)S(1)}, f32[1,2,8,1,128]{4,3,2,1,0:T(1,128)S(1)}, u32[]{:S(2)}, u32[]{:S(2)}) collective-permute-start(f32[1,2,8,1,128]{4,3,2,1,0:T(1,128)S(1)} %get-tuple-element.54), channel_id=1, source_target_pairs={{16,0},{32,16},{48,32},{64,48},{80,64},{96,80},{112,96},{128,112},... | collective-permute-start | bytes 24584 | tf_op jit(solution)/shard_map/ppermute | solution.py:18
  306.3 5.3 %collective-permute-start.19 = (f32[1,2,1,34,128]{4,3,2,1,0:T(8,128)S(1)}, f32[1,2,1,34,128]{4,3,2,1,0:T(8,128)S(1)}, u32[]{:S(2)}, u32[]{:S(2)}) collective-permute-start(f32[1,2,1,34,128]{4,3,2,1,0:T(8,128)S(1)} %get-tuple-element.42), channel_id=1, source_target_pairs={{1,0},{2,1},{3,2},{4,3},{5,4},{6,5},{7,6},{8,7},{9,8},{10,9},{11,1... | collective-permute-start | bytes 104456 | tf_op jit(solution)/shard_map/ppermute | solution.py:18
  312.3 9.3 %collective-permute-start.20 = (f32[1,2,8,1,128]{4,3,2,1,0:T(1,128)S(1)}, f32[1,2,8,1,128]{4,3,2,1,0:T(1,128)S(1)}, u32[]{:S(2)}, u32[]{:S(2)}) collective-permute-start(f32[1,2,8,1,128]{4,3,2,1,0:T(1,128)S(1)} %get-tuple-element.51), channel_id=1, source_target_pairs={{0,16},{16,32},{32,48},{48,64},{64,80},{80,96},{96,112},{112,128},... | collective-permute-start | bytes 24584 | tf_op jit(solution)/shard_map/ppermute | solution.py:17
  314.3 8.0 %collective-permute-start.21 = (f32[1,2,8,1,128]{4,3,2,1,0:T(1,128)S(1)}, f32[1,2,8,1,128]{4,3,2,1,0:T(1,128)S(1)}, u32[]{:S(2)}, u32[]{:S(2)}) collective-permute-start(f32[1,2,8,1,128]{4,3,2,1,0:T(1,128)S(1)} %get-tuple-element.52), channel_id=1, source_target_pairs={{16,0},{32,16},{48,32},{64,48},{80,64},{96,80},{112,96},{128,112},... | collective-permute-start | bytes 24584 | tf_op jit(solution)/shard_map/ppermute | solution.py:18
  325.1 5.3 %collective-permute-start.23 = (f32[1,2,1,34,128]{4,3,2,1,0:T(8,128)S(1)}, f32[1,2,1,34,128]{4,3,2,1,0:T(8,128)S(1)}, u32[]{:S(2)}, u32[]{:S(2)}) collective-permute-start(f32[1,2,1,34,128]{4,3,2,1,0:T(8,128)S(1)} %get-tuple-element.40), channel_id=1, source_target_pairs={{1,0},{2,1},{3,2},{4,3},{5,4},{6,5},{7,6},{8,7},{9,8},{10,9},{11,1... | collective-permute-start | bytes 104456 | tf_op jit(solution)/shard_map/ppermute | solution.py:18
  (11 other events, 260.9 us)
Sparse Core Ops, SparseCore 0:
  102.1 121.6 all-reduce.8
where the time goes:
time: 342 us; the launch traced here: 339 us
  waiting for transfers between devices  147 us (43%)
  starting transfers between devices  97.8 us (29%)
  other arithmetic  32.4 us (9%)
  local copies, waits for them, and re-layouts  21.4 us (6%)
  blocking collectives  18.2 us (5%)
  between operations  14 us (4%)
  matrix products  8.24 us (2%)
    psum x1, waiting for transfers between devices, body(): lax.psum(partial_value.astype(jnp.bfloat16), 'lev').astype(jnp.float32)  117 us
    ppermute x12, starting transfers between devices, padded_2(): after = lax.ppermute(leading, axis, down)  55.6 us
    ppermute x12, starting transfers between devices, padded_2(): before = lax.ppermute(last, axis, up)  35.2 us
    scatter-add x1, other arithmetic, body(): jnp.zeros((width, longs * lats), jnp.float32).at[:, col_index]  23.2 us
    ppermute x12, waiting for transfers between devices, padded_2(): after = lax.ppermute(leading, axis, down)  20.5 us
    all_to_all x1, blocking collectives, body(): lax.all_to_all(returned, 'band', split_axis=1, concat_axis=1, tiled=True)  18.2 us
    gather x2, local copies, waits for them, and re-layouts, body(): jnp.take(state.reshape(width, longs * lats), col_index, axis=1)  12.5 us
    all_to_all x1, waiting for transfers between devices, body(): lax.all_to_all(profile, 'band', split_axis=1, concat_axis=1, tiled=True)  9.04 us
  transfers between devices with their start and end apart: 26, of which 13 were waited for; matrix products, arithmetic and copies ran while one was open for 1% of the time, Pallas kernels for 0%

commit v1 on v0

v1 whole, which is shorter than its diff:
```python
import functools

import jax
import jax.numpy as jnp
from jax import lax
from jax.experimental import pallas as pl
from jax.experimental.pallas import tpu as pltpu
from jax.sharding import PartitionSpec as P

MESH = pl.DeviceIdType.MESH
F32 = jnp.float32
BF16 = jnp.bfloat16

NTAB = 4
STEPS = 3
HALO = 3
FIELDS = 2
LEV = 8
LON = 32
LAT = 128
CAP = 128
ROWS = LON + 8
EXT = LEV + 2 * HALO
WIDTH = FIELDS * LEV
PAIR = 2 * CAP


def dot(a, b, dims):
    return lax.dot_general(a, b, (dims, ((), ())), preferred_element_type=F32)


def kernel(
    nb,
    ng,
    inc_hbm,
    dif_hbm,
    sig_hbm,
    jac_hbm,
    rinv_ref,
    inn_hbm,
    col_hbm,
    tab_hbm,
    cnt_ref,
    out_ref,
    inc_e,
    dif_e,
    sig_v,
    col_v,
    tab_v,
    inn_v,
    inn_f,
    inn_s,
    pack,
    lon_r,
    pack_w,
    lon_w,
    w_e,
    dfx,
    ua,
    ub,
    uc,
    st,
    s_mat,
    hot,
    a_mat,
    adj,
    prof,
    arr,
    junk,
    tabs,
    tabs_t,
    rcol,
    back,
    home,
    load_sem,
    halo_send,
    halo_recv,
    w_send,
    w_recv,
    tab_sem,
    x_sem,
):
    b, g = lax.axis_index("band"), lax.axis_index("lev")
    per = nb // ng
    nz = ng // 2
    z, core = g // 2, g % 2
    left, right = lax.rem(b + nb - 1, nb), lax.rem(b + 1, nb)
    hub = b // per
    has_low, has_high = g > 0, g < ng - 1

    loads = [
        pltpu.make_async_copy(inc_hbm, inc_e.at[:, HALO : HALO + LEV], load_sem.at[0]),
        pltpu.make_async_copy(dif_hbm, dif_e.at[:, HALO : HALO + LEV], load_sem.at[1]),
        pltpu.make_async_copy(sig_hbm, sig_v, load_sem.at[2]),
        pltpu.make_async_copy(col_hbm.at[0], col_v, load_sem.at[3]),
        pltpu.make_async_copy(tab_hbm.at[0], tab_v, load_sem.at[4]),
        pltpu.make_async_copy(
            inn_hbm.at[0, :, pl.ds(pl.multiple_of((per * g) // 16 * 16, 16), 16)],
            inn_v,
            load_sem.at[5],
        ),
    ]
    for load in loads:
        load.start()

    barrier = pltpu.get_barrier_semaphore()

    def greet(band, lev):
        pl.semaphore_signal(barrier, inc=1, device_id=(band, lev), device_id_type=MESH)

    for side in (left, right):
        greet(side, g)
    for has, lev in ((has_low, g - 1), (has_high, g + 1)):

        @pl.when(has)
        def _():
            for side in (left, b, right):
                greet(side, lev)

    @pl.loop(0, nz)
    def _(other):
        @pl.when(other != z)
        def _():
            greet(b, 2 * other + core)

    @pl.loop(0, per * ng)
    def _(index):
        band, lev = per * g + index // ng, index % ng

        @pl.when(jnp.logical_or(band != b, lev != g))
        def _():
            greet(band, lev)

    zeros = jnp.zeros((FIELDS, HALO, LON, LAT), BF16)

    @pl.when(g == 0)
    def _():
        inc_e[:, 0:HALO] = zeros
        dif_e[:, 0:HALO] = zeros
        w_e[:, 0:HALO] = zeros
        lon_r[:, 0:HALO] = jnp.zeros((2, HALO, 16, LAT), BF16)
        lon_w[:, 0:HALO] = jnp.zeros((2, HALO, 16, LAT), BF16)

    @pl.when(g == ng - 1)
    def _():
        inc_e[:, EXT - HALO :] = zeros
        dif_e[:, EXT - HALO :] = zeros
        w_e[:, EXT - HALO :] = zeros
        lon_r[:, EXT - HALO :] = jnp.zeros((2, HALO, 16, LAT), BF16)
        lon_w[:, EXT - HALO :] = jnp.zeros((2, HALO, 16, LAT), BF16)

    for e in (0, EXT - 1):
        lon_r[:, e] = jnp.zeros((2, 16, LAT), BF16)
        lon_w[:, e] = jnp.zeros((2, 16, LAT), BF16)

    sub = lax.broadcasted_iota(jnp.int32, (8, LAT), 0)
    upper = sub < 4
    loads[0].wait()
    loads[1].wait()

    def pack_level(l):
        for side in (0, 1):
            tiles = []
            for f in range(FIELDS):
                x = inc_e[f, HALO + l].astype(F32)
                d = dif_e[f, HALO + l].astype(F32)
                if side == 0:
                    tile = jnp.where(upper, x[0:8], pltpu.roll(d[0:8], 4, 0))
                else:
                    tile = jnp.where(upper, pltpu.roll(d[LON - 8 :], 4, 0), x[LON - 8 :])
                tiles.append(tile)
            pack[side, l] = jnp.concatenate(tiles, axis=0).astype(BF16)

    pl.loop(0, LEV)(pack_level)

    senders = (
        2
        + 3 * has_low.astype(jnp.int32)
        + 3 * has_high.astype(jnp.int32)
        + (nz - 1)
        + nb
        - (g == hub).astype(jnp.int32)
    )
    pl.semaphore_wait(barrier, senders)

    def halo_copies(strips, lon_to, lev_pairs, send, recv):
        def copy(k, src, dst, band, lev):
            return pltpu.make_async_remote_copy(
                src_ref=src,
                dst_ref=dst,
                send_sem=send.at[k],
                recv_sem=recv.at[k],
                device_id=(band, lev),
                device_id_type=MESH,
            )

        level, up, down = [], [], []
        sides = (left, right)
        for k in (0, 1):
            level.append(copy(k, strips.at[k], lon_to.at[k, HALO : HALO + LEV], sides[k], g))
            up.append(copy(2 + k, strips.at[k, LEV - 2 :], lon_to.at[k, 1:HALO], sides[k], g + 1))
            down.append(
                copy(4 + k, strips.at[k, 0:2], lon_to.at[k, EXT - HALO : EXT - 1], sides[k], g - 1)
            )
        for i, (src, base, dst) in enumerate(lev_pairs):
            up.append(
                copy(6 + i, src.at[:, base + LEV - HALO : base + LEV], dst.at[:, 0:HALO], b, g + 1)
            )
            down.append(
                copy(8 + i, src.at[:, base : base + HALO], dst.at[:, EXT - HALO :], b, g - 1)
            )
        return level, up, down

    def halo_start(level, up, down):
        for has, copies in ((has_high, up), (has_low, down)):

            @pl.when(has)
            def _():
                for c in reversed(copies):
                    c.start()

        for c in level:
            c.start()

    def halo_arrive(level, up, down):
        for c in level:
            c.wait_recv()
        for has, copies in ((has_low, up), (has_high, down)):

            @pl.when(has)
            def _():
                for c in copies:
                    c.wait_recv()

    def halo_sent(level, up, down):
        for c in level:
            c.wait_send()
        for has, copies in ((has_high, up), (has_low, down)):

            @pl.when(has)
            def _():
                for c in copies:
                    c.wait_send()

    halo = halo_copies(
        pack, lon_r, ((inc_hbm, 0, inc_e), (dif_hbm, 0, dif_e)), halo_send, halo_recv
    )
    halo_start(*halo)

    own_tab = pltpu.make_async_copy(jac_hbm, tabs.at[core, z], tab_sem.at[1])
    own_tab.start()

    @pl.loop(0, nz)
    def _(other):
        @pl.when(other != z)
        def _():
            pltpu.make_async_remote_copy(
                src_ref=jac_hbm,
                dst_ref=tabs.at[core, z],
                send_sem=tab_sem.at[0],
                recv_sem=tab_sem.at[1],
                device_id=(b, 2 * other + core),
                device_id_type=MESH,
            ).start()

    loads[3].wait()

    def col_row(i):
        return jnp.concatenate([col_v[pl.ds(2 * i, 1)], col_v[pl.ds(2 * i + 1, 1)]], axis=1)

    def lon_low(cols):
        return lax.shift_right_logical(cols, 7) & 15

    def build_hot(i):
        cols = col_row(i)
        want = (lax.shift_right_logical(cols, 11) & 1) * LAT + (cols & (LAT - 1))
        iota = lax.broadcasted_iota(jnp.int32, (2 * LAT, PAIR), 0)
        hot[:, pl.ds(pl.multiple_of(i * PAIR, PAIR), PAIR)] = jnp.where(
            iota == want, 1.0, 0.0
        ).astype(BF16)

    pl.loop(0, nb // 2)(build_hot)

    halo_arrive(*halo)

    def widen(f, e):
        first = lon_r[0, e].astype(F32)
        last = lon_r[1, e].astype(F32)
        for k in range(FIELDS):

            @pl.when(f == k)
            def _():
                r = first[8 * k : 8 * k + 8]
                l = last[8 * k : 8 * k + 8]
                ua[k, e, LON:] = jnp.where(upper, r, l)
                dfx[k, e, LON:] = pltpu.roll(jnp.where(upper, l, r), 4, 0)

        ua[f, e, 0:LON] = inc_e[f, e].astype(F32)
        dfx[f, e, 0:LON] = dif_e[f, e].astype(F32)

    for f in range(FIELDS):
        pl.loop(0, EXT)(functools.partial(widen, f))

    lane = lax.broadcasted_iota(jnp.int32, (ROWS, LAT), 1)

    def lap(ref, f, e):
        c = ref[f, e]
        total = ref[f, e - 1] + ref[f, e + 1]
        total = total + (pltpu.roll(c, 1, 0) + pltpu.roll(c, ROWS - 1, 0))
        total = total + jnp.where(lane == 0, 0.0, pltpu.roll(c, 1, 1))
        total = total + jnp.where(lane == LAT - 1, 0.0, pltpu.roll(c, LAT - 1, 1))
        return total - 6.0 * c

    def forward(src, dst, step):
        def body(e):
            for f in range(FIELDS):
                dst[f, e] = src[f, e] + dfx[f, e] * lap(src, f, e)

        pl.loop(step, EXT - step)(body)

    forward(ua, ub, 1)
    forward(ub, ua, 2)
    loads[2].wait()

    def last_step(l):
        for f in range(FIELDS):
            e = l + HALO
            field = (ua[f, e] + dfx[f, e] * lap(ua, f, e))[0:LON]
            st[pl.ds(pl.multiple_of((f * LEV + l) * LON, LON), LON)] = (
                sig_v[f, l].astype(F32) * field
            )

    pl.loop(0, LEV)(last_step)

    for lon in range(LON):
        parts = [st[pl.ds(f * LEV * LON + lon, LEV, stride=LON)] for f in range(FIELDS)]
        s_mat[
            (lon % 16) * WIDTH : (lon % 16 + 1) * WIDTH, (lon // 16) * LAT : (lon // 16 + 1) * LAT
        ] = jnp.concatenate(parts, axis=0).astype(BF16)

    def gather(i):
        cols = col_row(i)
        low = lon_low(cols)
        chunk = hot[:, pl.ds(pl.multiple_of(i * PAIR, PAIR), PAIR)]
        rows = dot(s_mat[...], chunk, ((1,), (0,)))
        total = jnp.zeros((WIDTH, PAIR), F32)
        for k in range(16):
            total = jnp.where(low == k, rows[k * WIDTH : (k + 1) * WIDTH], total)
        total = total.astype(BF16)
        for half in range(2):
            owner = 2 * i + half
            prof[owner] = total[:, half * CAP : (half + 1) * CAP]
            here = jnp.logical_and(owner == b, g == hub)
            slot = arr.at[b % per, core, z]

            @pl.when(here)
            def _():
                pltpu.make_async_copy(prof.at[owner], slot, x_sem.at[1]).start()
                pltpu.make_async_copy(prof.at[owner], junk.at[0], x_sem.at[0]).start()

            @pl.when(jnp.logical_not(here))
            def _():
                pltpu.make_async_remote_copy(
                    src_ref=prof.at[owner],
                    dst_ref=slot,
                    send_sem=x_sem.at[0],
                    recv_sem=x_sem.at[1],
                    device_id=(owner, hub),
                    device_id_type=MESH,
                ).start()

    pl.loop(0, nb // 2)(gather)

    pltpu.make_async_copy(tabs.at[0], tabs.at[0], tab_sem.at[1]).wait()
    share = pltpu.make_async_remote_copy(
        src_ref=tabs.at[core],
        dst_ref=tabs.at[core],
        send_sem=tab_sem.at[2],
        recv_sem=tab_sem.at[3],
        device_id=(b, g + 1 - 2 * core),
        device_id_type=MESH,
    )
    share.start()

    loads[5].wait()
    loads[4].wait()

    def spread_inn(i):
        at = pl.ds(pl.multiple_of(i * 8, 8), 8)
        inn_f[pl.ds(pl.multiple_of(i * 128, 128), 128)] = (
            inn_v[at].astype(F32).reshape(128, CAP)
        )

    channels = inn_v.shape[0]
    pl.loop(0, channels // 8)(spread_inn)
    row = lax.rem(per * g, 16)
    for j in range(per):
        for i in range(channels // 8):
            inn_s[8 * i : 8 * i + 8, j * CAP : (j + 1) * CAP] = inn_f[
                pl.ds(i * 128 + row + j, 8, stride=16)
            ]
    for i in range(channels // 128):
        line = rinv_ref[:, i * 128 : (i + 1) * 128]
        rcol[i * 128 : (i + 1) * 128] = jnp.broadcast_to(line, (128, 128)).T

    pltpu.make_async_copy(tabs.at[0], tabs.at[0], tab_sem.at[3]).wait()

    def table(t):
        return tabs[:, :, t].reshape(ng * WIDTH, channels)

    for t in range(NTAB):
        tabs_t[t] = table(t).T

    pltpu.make_async_copy(arr, arr, x_sem.at[1]).wait()
    profiles = jnp.concatenate(
        [arr[j].reshape(ng * WIDTH, CAP) for j in range(per)], axis=1
    )
    kinds = jnp.concatenate([tab_v[pl.ds(per * g + j, 1)] for j in range(per)], axis=1)
    slot_id = lax.broadcasted_iota(jnp.int32, (1, CAP), 1)
    valid = jnp.concatenate(
        [(slot_id < cnt_ref[0, per * g + j]).astype(jnp.int32) for j in range(per)], axis=1
    )
    evolved = jnp.zeros((channels, per * CAP), F32)
    for t in range(NTAB):
        evolved = jnp.where(kinds == t, dot(tabs_t[t], profiles, ((1,), (0,))), evolved)
    scale = jnp.concatenate([rcol[...]] * per, axis=1)
    resid = jnp.where(valid > 0, scale * (evolved - inn_s[...]), 0.0)
    total = jnp.zeros((ng * WIDTH, per * CAP), F32)
    for t in range(NTAB):
        masked = jnp.where(kinds == t, resid, 0.0).astype(BF16)
        total = total + dot(table(t), masked, ((1,), (0,)))
    for j in range(per):
        back[j] = (
            total[:, j * CAP : (j + 1) * CAP].astype(BF16).reshape(2, nz, WIDTH, CAP)
        )

    @pl.loop(0, per * ng)
    def _(index):
        j, lev = index // ng, index % ng
        band = per * g + j
        here = jnp.logical_and(band == b, lev == g)
        src = back.at[j, lev % 2, lev // 2]

        @pl.when(here)
        def _():
            pltpu.make_async_copy(src, home.at[b], x_sem.at[3]).start()
            pltpu.make_async_copy(src, junk.at[1], x_sem.at[2]).start()

        @pl.when(jnp.logical_not(here))
        def _():
            pltpu.make_async_remote_copy(
                src_ref=src,
                dst_ref=home.at[b],
                send_sem=x_sem.at[2],
                recv_sem=x_sem.at[3],
                device_id=(band, lev),
                device_id_type=MESH,
            ).start()

    pltpu.make_async_copy(home, home, x_sem.at[3]).wait()

    def spread_home(i):
        low = lon_low(col_row(i))
        block = jnp.concatenate([home[2 * i], home[2 * i + 1]], axis=1).astype(F32)
        at = pl.ds(pl.multiple_of(i * PAIR, PAIR), PAIR)
        for k in range(16):
            a_mat[k * WIDTH : (k + 1) * WIDTH, at] = jnp.where(low == k, block, 0.0).astype(BF16)

    pl.loop(0, nb // 2)(spread_home)
    sums = dot(a_mat[...], hot[...], ((1,), (1,)))
    for k in range(2):
        adj[k * 256 : (k + 1) * 256] = sums[:, k * LAT : (k + 1) * LAT]

    for l in range(LEV):
        firsts, lasts = [], []
        for f in range(FIELDS):
            for i in range(LON // 8):
                cells = adj[pl.ds(i * 8 * WIDTH + f * LEV + l, 8, stride=WIDTH)]
                w = sig_v[f, l, 8 * i : 8 * i + 8].astype(F32) * cells
                ua[f, HALO + l, 8 * i : 8 * i + 8] = w
                if i == 0:
                    firsts.append(w)
                if i == LON // 8 - 1:
                    lasts.append(w)
        pack_w[0, l] = jnp.concatenate(firsts, axis=0).astype(BF16)
        pack_w[1, l] = jnp.concatenate(lasts, axis=0).astype(BF16)
        for f in range(FIELDS):
            w_e[f, HALO + l] = ua[f, HALO + l, 0:LON].astype(BF16)

    halo2 = halo_copies(pack_w, lon_w, ((w_e, HALO, w_e),), w_send, w_recv)
    halo_start(*halo2)
    halo_arrive(*halo2)

    def widen_w(e):
        first = lon_w[0, e].astype(F32)
        last = lon_w[1, e].astype(F32)
        for f in range(FIELDS):
            ua[f, e, LON:] = jnp.where(upper, first[8 * f : 8 * f + 8], last[8 * f : 8 * f + 8])

    pl.loop(0, EXT)(widen_w)
    for f in range(FIELDS):
        for e in (0, 1, 2, EXT - 3, EXT - 2, EXT - 1):
            ua[f, e, 0:LON] = w_e[f, e].astype(F32)

    def scale_all(e):
        for f in range(FIELDS):
            ub[f, e] = dfx[f, e] * ua[f, e]

    pl.loop(0, EXT)(scale_all)

    def backward(src, dst, step):
        def body(e):
            for f in range(FIELDS):
                w = ua[f, e] + lap(src, f, e)
                ua[f, e] = w
                dst[f, e] = dfx[f, e] * w

        pl.loop(step, EXT - step)(body)

    backward(ub, uc, 1)
    backward(uc, ub, 2)

    def finish(l):
        for f in range(FIELDS):
            e = l + HALO
            w = (ua[f, e] + lap(ub, f, e))[0:LON]
            out_ref[f, l] = inc_e[f, e].astype(F32) + w

    pl.loop(0, LEV)(finish)

    halo_sent(*halo)
    halo_sent(*halo2)
    if nz > 1:
        gone = tabs.at[0, 0 : nz - 1]
        pltpu.make_async_copy(gone, gone, tab_sem.at[0]).wait()
    share.wait_send()
    pltpu.make_async_copy(prof, prof, x_sem.at[0]).wait()
    pltpu.make_async_copy(back, back, x_sem.at[2]).wait()


def body(
    nb,
    ng,
    increment,
    diffusivity,
    sigma,
    jacobian,
    rinv,
    innovation,
    obs_column,
    obs_table,
    obs_count,
):
    channels = jacobian.shape[1]
    tables = jnp.transpose(jacobian, (0, 2, 3, 1)).reshape(NTAB, WIDTH, channels)
    per, nz = nb // ng, ng // 2
    hbm = pl.BlockSpec(memory_space=pl.ANY)
    vmem = pl.BlockSpec(memory_space=pltpu.VMEM)
    smem = pl.BlockSpec(memory_space=pltpu.SMEM)
    dma = pltpu.SemaphoreType.DMA
    extended = pltpu.VMEM((FIELDS, EXT, LON, LAT), BF16)
    wide = pltpu.VMEM((FIELDS, EXT, ROWS, LAT), F32)
    return pl.pallas_call(
        functools.partial(kernel, nb, ng),
        out_shape=jax.ShapeDtypeStruct((FIELDS, LEV, LON, LAT), F32),
        in_specs=[hbm, hbm, hbm, hbm, vmem, hbm, hbm, hbm, smem],
        out_specs=vmem,
        scratch_shapes=[
            extended,
            extended,
            pltpu.VMEM((FIELDS, LEV, LON, LAT), BF16),
            pltpu.VMEM((nb, CAP), jnp.int32),
            pltpu.VMEM((nb, CAP), jnp.int32),
            pltpu.VMEM((channels, 16, CAP), BF16),
            pltpu.VMEM((channels * 16, CAP), F32),
            pltpu.VMEM((channels, per * CAP), F32),
            pltpu.VMEM((2, LEV, 16, LAT), BF16),
            pltpu.VMEM((2, EXT, 16, LAT), BF16),
            pltpu.VMEM((2, LEV, 16, LAT), BF16),
            pltpu.VMEM((2, EXT, 16, LAT), BF16),
            extended,
            wide,
            wide,
            wide,
            wide,
            pltpu.VMEM((WIDTH * LON, LAT), F32),
            pltpu.VMEM((16 * WIDTH, 2 * LAT), BF16),
            pltpu.VMEM((2 * LAT, nb * CAP), BF16),
            pltpu.VMEM((16 * WIDTH, nb * CAP), BF16),
            pltpu.VMEM((WIDTH * LON, LAT), F32),
            pltpu.VMEM((nb, WIDTH, CAP), BF16),
            pltpu.VMEM((per, 2, nz, WIDTH, CAP), BF16),
            pltpu.VMEM((2, WIDTH, CAP), BF16),
            pltpu.VMEM((2, nz, NTAB, WIDTH, channels), BF16),
            pltpu.VMEM((NTAB, channels, ng * WIDTH), BF16),
            pltpu.VMEM((channels, CAP), F32),
            pltpu.VMEM((per, 2, nz, WIDTH, CAP), BF16),
            pltpu.VMEM((nb, WIDTH, CAP), BF16),
            dma((6,)),
            dma((10,)),
            dma((10,)),
            dma((10,)),
            dma((10,)),
            dma((4,)),
            dma((4,)),
        ],
        compiler_params=pltpu.CompilerParams(
            collective_id=0, has_side_effects=True, vmem_limit_bytes=48 * 1024 * 1024
        ),
    )(
        increment,
        diffusivity,
        sigma,
        tables,
        rinv.reshape(1, channels),
        innovation,
        obs_column,
        obs_table,
        obs_count,
    )


def solution(mesh):
    in_specs = (
        P(None, "lev", "band", None),
        P(None, "lev", "band", None),
        P(None, "lev", "band", None),
        P(None, None, None, "lev"),
        P(),
        P("band", None, None, None),
        P("band", None, None),
        P("band", None, None),
        P("band", None),
    )
    out_specs = P(None, "lev", "band", None)
    run = functools.partial(body, mesh.shape["band"], mesh.shape["lev"])
    return jax.shard_map(run, mesh=mesh, in_specs=in_specs, out_specs=out_specs, check_vma=False)
```

time: 342 us -> 67 us (0.20)
  waiting for transfers between devices: 147 us -> 0 us
  starting transfers between devices: 97.8 us -> 0 us
  Pallas kernels: 0 us -> 58 us
  other arithmetic: 32.4 us -> 0 us
  blocking collectives: 18.2 us -> 0 us
  between operations: 14 us -> 0.02 us
  local copies, waits for them, and re-layouts: 21.4 us -> 8.53 us
  matrix products: 8.24 us -> 0 us
    psum x1 -> x0, waiting for transfers between devices: 117 us -> none  [body(): lax.psum(partial_value.astype(jnp.bfloat16), 'lev').astype(jnp.float32)]
    ppermute x24 -> x0, starting transfers between devices: 90.8 us -> none  [the longest x12 55.6 us: padded_2(): after = lax.ppermute(leading, axis, down)]
    pallas_call x0 -> x1, Pallas kernels: none -> 58 us  [body(): pl.pallas_call(functools.partial(kernel, nb, ng), out_shape=jax.ShapeDtyp...]
    scatter-add x1 -> x0, other arithmetic: 23.2 us -> none  [body(): jnp.zeros((width, longs * lats), jnp.float32).at[:, col_index]]
    ppermute x24 -> x0, waiting for transfers between devices: 20.5 us -> none  [the longest x12 20.5 us: padded_2(): after = lax.ppermute(leading, axis, down)]
    all_to_all x1 -> x0, blocking collectives: 18.2 us -> none  [body(): lax.all_to_all(returned, 'band', split_axis=1, concat_axis=1, tiled=True)]
    gather x2 -> x0, local copies, waits for them, and re-layouts: 12.5 us -> none  [body(): jnp.take(state.reshape(width, longs * lats), col_index, axis=1)]
    all_to_all x1 -> x0, waiting for transfers between devices: 9.04 us -> none  [body(): lax.all_to_all(profile, 'band', split_axis=1, concat_axis=1, tiled=True)]
  transfers between devices with their start and end apart: 26 -> 0, of which waited for: 13 -> 0; matrix products, arithmetic and copies ran while one was open for 1% -> 0% of each run, Pallas kernels for 0% -> 0%
where the time goes in v1:
time: 67 us; the launch traced here: 66.6 us
  Pallas kernels  58 us (87%)
  local copies, waits for them, and re-layouts  8.53 us (13%)
    pallas_call x1, Pallas kernels, body(): pl.pallas_call(functools.partial(kernel, nb, ng), out_shape=jax.ShapeDtyp...  58 us
    unnamed x19, local copies, waits for them, and re-layouts  8.53 us

profile of v1, /device:TPU:1, one launch (start us, length us, event | category | flops | bytes accessed | tf_op | source)
XLA Modules:
  0.0 66.6 jit_solution(12514219506751124180)
XLA Ops:
  0.0 0.0 copy-start
  0.0 1.6 %copy-done = bf16[1,256,32,128]{3,2,1,0:T(8,128)(2,1)S(1)} copy-done((bf16[1,256,32,128]{3,2,1,0:T(8,128)(2,1)S(1)}, bf16[1,256,32,128]{3,2,1,0:T(8,128)(2,1)}, u32[]{:S(2)}) %copy-start) | copy-done | bytes 2097176
  1.6 0.0 copy-start.1
  1.6 0.9 %copy-done.1 = bf16[2,8,32,128]{3,2,1,0:T(8,128)(2,1)S(1)} copy-done((bf16[2,8,32,128]{3,2,1,0:T(8,128)(2,1)S(1)}, bf16[2,8,32,128]{3,2,1,0:T(8,128)(2,1)}, u32[]{:S(2)}) %copy-start.1) | copy-done | bytes 131096
  2.5 0.0 copy-start.2
  2.5 0.9 %copy-done.2 = bf16[2,8,32,128]{3,2,1,0:T(8,128)(2,1)S(1)} copy-done((bf16[2,8,32,128]{3,2,1,0:T(8,128)(2,1)S(1)}, bf16[2,8,32,128]{3,2,1,0:T(8,128)(2,1)}, u32[]{:S(2)}) %copy-start.2) | copy-done | bytes 131096
  3.4 0.0 copy-start.3
  3.4 0.9 %copy-done.3 = bf16[2,8,32,128]{3,2,1,0:T(8,128)(2,1)S(1)} copy-done((bf16[2,8,32,128]{3,2,1,0:T(8,128)(2,1)S(1)}, bf16[2,8,32,128]{3,2,1,0:T(8,128)(2,1)}, u32[]{:S(2)}) %copy-start.3) | copy-done | bytes 131096
  4.3 0.0 copy-start.4
  4.3 0.8 %copy-done.4 = bf16[4,256,2,8]{1,3,2,0:T(8,128)(2,1)S(1)} copy-done((bf16[4,256,2,8]{1,3,2,0:T(8,128)(2,1)S(1)}, bf16[4,256,2,8]{1,3,2,0:T(8,128)(2,1)}, u32[]{:S(2)}) %copy-start.4) | copy-done | bytes 32792
  5.1 0.0 copy-start.5
  5.1 0.7 %copy-done.5 = s32[1,32,128]{2,1,0:T(8,128)S(1)} copy-done((s32[1,32,128]{2,1,0:T(8,128)S(1)}, s32[1,32,128]{2,1,0:T(8,128)}, u32[]{:S(2)}) %copy-start.5) | copy-done | bytes 16408
  5.8 0.0 copy-start.6
  5.8 0.7 %copy-done.6 = s32[1,32,128]{2,1,0:T(8,128)S(1)} copy-done((s32[1,32,128]{2,1,0:T(8,128)S(1)}, s32[1,32,128]{2,1,0:T(8,128)}, u32[]{:S(2)}) %copy-start.6) | copy-done | bytes 16408
  6.5 0.0 copy-start.7
  6.5 0.7 %copy-done.7 = f32[256]{0:T(256)S(1)} copy-done((f32[256]{0:T(256)S(1)}, f32[256]{0:T(256)}, u32[]{:S(2)}) %copy-start.7) | copy-done | bytes 1048
  7.2 0.0 copy-start.8
  7.2 0.7 copy-done.8
  7.8 58.0 %shard_map.91 = f32[2,8,32,128]{3,2,1,0:T(8,128)S(1)} custom-call(bf16[2,8,32,128]{3,2,1,0:T(8,128)(2,1)S(1)} %copy-done.1, bf16[2,8,32,128]{3,2,1,0:T(8,128)(2,1)S(1)} %copy-done.2, bf16[2,8,32,128]{3,2,1,0:T(8,128)(2,1)S(1)} %copy-done.3, bf16[4,16,256]{2,1,0:T(8,128)(2,1)S(1)} %bitcast.4, f32[1,256]{1,0:T(1,128)S(1)} %bitcast.5, ...), custom_call_target="tpu_custom_call" | custom-call | tf_op jit(solution)/shard_map/pallas_call | solution.py:563
  65.9 0.7 %copy.11 = f32[2,8,32,128]{3,2,1,0:T(8,128)} copy(f32[2,8,32,128]{3,2,1,0:T(8,128)S(1)} %shard_map.91) | data formatting | bytes 524288
Async XLA Ops:
  0.0 1.6 %copy-start = (bf16[1,256,32,128]{3,2,1,0:T(8,128)(2,1)S(1)}, bf16[1,256,32,128]{3,2,1,0:T(8,128)(2,1)}, u32[]{:S(2)}) copy-start(bf16[1,256,32,128]{3,2,1,0:T(8,128)(2,1)} %inn_hbm.1) | copy-start | bytes 6291460
  1.6 0.9 %copy-start.1 = (bf16[2,8,32,128]{3,2,1,0:T(8,128)(2,1)S(1)}, bf16[2,8,32,128]{3,2,1,0:T(8,128)(2,1)}, u32[]{:S(2)}) copy-start(bf16[2,8,32,128]{3,2,1,0:T(8,128)(2,1)} %inc_hbm.1) | copy-start | bytes 393220
  2.5 0.9 %copy-start.2 = (bf16[2,8,32,128]{3,2,1,0:T(8,128)(2,1)S(1)}, bf16[2,8,32,128]{3,2,1,0:T(8,128)(2,1)}, u32[]{:S(2)}) copy-start(bf16[2,8,32,128]{3,2,1,0:T(8,128)(2,1)} %dif_hbm.1) | copy-start | bytes 393220
  3.4 0.9 %copy-start.3 = (bf16[2,8,32,128]{3,2,1,0:T(8,128)(2,1)S(1)}, bf16[2,8,32,128]{3,2,1,0:T(8,128)(2,1)}, u32[]{:S(2)}) copy-start(bf16[2,8,32,128]{3,2,1,0:T(8,128)(2,1)} %sig_hbm.1) | copy-start | bytes 393220
  4.3 0.8 %copy-start.4 = (bf16[4,256,2,8]{1,3,2,0:T(8,128)(2,1)S(1)}, bf16[4,256,2,8]{1,3,2,0:T(8,128)(2,1)}, u32[]{:S(2)}) copy-start(bf16[4,256,2,8]{1,3,2,0:T(8,128)(2,1)} %param.12) | copy-start | bytes 98308
  5.1 0.7 %copy-start.5 = (s32[1,32,128]{2,1,0:T(8,128)S(1)}, s32[1,32,128]{2,1,0:T(8,128)}, u32[]{:S(2)}) copy-start(s32[1,32,128]{2,1,0:T(8,128)} %col_hbm.1) | copy-start | bytes 49156
  5.8 0.7 %copy-start.6 = (s32[1,32,128]{2,1,0:T(8,128)S(1)}, s32[1,32,128]{2,1,0:T(8,128)}, u32[]{:S(2)}) copy-start(s32[1,32,128]{2,1,0:T(8,128)} %tab_hbm.1) | copy-start | bytes 49156
  6.5 0.7 %copy-start.7 = (f32[256]{0:T(256)S(1)}, f32[256]{0:T(256)}, u32[]{:S(2)}) copy-start(f32[256]{0:T(256)} %param.13) | copy-start | bytes 3076
  7.2 0.7 copy-start.8

commit v2 on v1

v2 whole, which is shorter than its diff:
```python
import functools

import jax
import jax.numpy as jnp
from jax import lax
from jax.experimental import pallas as pl
from jax.experimental.pallas import tpu as pltpu
from jax.sharding import PartitionSpec as P

MESH = pl.DeviceIdType.MESH
F32 = jnp.float32
BF16 = jnp.bfloat16

NTAB = 4
STEPS = 3
HALO = 3
FIELDS = 2
LEV = 8
LON = 32
LAT = 128
CAP = 128
ROWS = LON + 8
EXT = LEV + 2 * HALO
WIDTH = FIELDS * LEV
PAIR = 2 * CAP


def dot(a, b, dims):
    return lax.dot_general(a, b, (dims, ((), ())), preferred_element_type=F32)


def run(step, work):
    work()


def kernel(
    nb,
    ng,
    inc_hbm,
    dif_hbm,
    sig_hbm,
    jac_hbm,
    rinv_hbm,
    inn_hbm,
    col_hbm,
    tab_hbm,
    cnt_hbm,
    out_hbm,
    out_v,
    inc_e,
    dif_e,
    sig_v,
    rinv_v,
    cnt_s,
    col_v,
    tab_v,
    inn_v,
    inn_f,
    inn_s,
    pack,
    lon_r,
    pack_w,
    lon_w,
    w_e,
    dfx,
    ua,
    ub,
    uc,
    st,
    s_mat,
    hot,
    a_mat,
    adj,
    prof,
    arr,
    junk,
    tabs,
    tabs_t,
    rcol,
    back,
    home,
    load_sem,
    halo_send,
    halo_recv,
    w_send,
    w_recv,
    tab_sem,
    x_sem,
):
    b, g = lax.axis_index("band"), lax.axis_index("lev")
    per = nb // ng
    nz = ng // 2
    z, core = g // 2, g % 2
    left, right = lax.rem(b + nb - 1, nb), lax.rem(b + 1, nb)
    hub = b // per
    has_low, has_high = g > 0, g < ng - 1
    channels = inn_v.shape[0]
    inn_rows = inn_v.shape[1]

    loads = [
        pltpu.make_async_copy(inc_hbm, inc_e.at[:, HALO : HALO + LEV], load_sem.at[0]),
        pltpu.make_async_copy(dif_hbm, dif_e.at[:, HALO : HALO + LEV], load_sem.at[1]),
        pltpu.make_async_copy(col_hbm.at[0], col_v, load_sem.at[2]),
        pltpu.make_async_copy(sig_hbm, sig_v, load_sem.at[3]),
        pltpu.make_async_copy(tab_hbm.at[0], tab_v, load_sem.at[4]),
        pltpu.make_async_copy(rinv_hbm, rinv_v, load_sem.at[5]),
        pltpu.make_async_copy(cnt_hbm, cnt_s, load_sem.at[6]),
        pltpu.make_async_copy(
            inn_hbm.at[
                0,
                :,
                pl.ds(pl.multiple_of((per * g) // inn_rows * inn_rows, inn_rows), inn_rows),
            ],
            inn_v,
            load_sem.at[7],
        ),
    ]
    l_inc, l_dif, l_col, l_sig, l_tab, l_rinv, l_cnt, l_inn = loads

    barrier = pltpu.get_barrier_semaphore()

    def greet(band, lev):
        pl.semaphore_signal(barrier, inc=1, device_id=(band, lev), device_id_type=MESH)

    def comm_greet():
        for side in (left, right):
            greet(side, g)
        for has, lev in ((has_low, g - 1), (has_high, g + 1)):

            @pl.when(has)
            def _():
                for side in (left, b, right):
                    greet(side, lev)

        @pl.loop(0, nz)
        def _(other):
            @pl.when(other != z)
            def _():
                greet(b, 2 * other + core)

        @pl.loop(0, per * ng)
        def _(index):
            band, lev = per * g + index // ng, index % ng

            @pl.when(jnp.logical_or(band != b, lev != g))
            def _():
                greet(band, lev)

    run(0, comm_greet)

    def start_loads():
        for load in loads:
            load.start()

    run(0, start_loads)

    zeros = jnp.zeros((FIELDS, HALO, LON, LAT), BF16)
    zeros_lon = jnp.zeros((2, HALO, 16, LAT), BF16)

    def clear():
        for edge, at in ((0, slice(0, HALO)), (ng - 1, slice(EXT - HALO, EXT))):

            @pl.when(g == edge)
            def _():
                inc_e[:, at] = zeros
                dif_e[:, at] = zeros
                w_e[:, at] = zeros
                lon_r[:, at] = zeros_lon
                lon_w[:, at] = zeros_lon

        for e in (0, EXT - 1):
            lon_r[:, e] = zeros_lon[:, 0]
            lon_w[:, e] = zeros_lon[:, 0]

    run(0, clear)

    sub = lax.broadcasted_iota(jnp.int32, (8, LAT), 0)
    upper = sub < 4

    def pack_level(l):
        for side in (0, 1):
            tiles = []
            for f in range(FIELDS):
                x = inc_e[f, HALO + l].astype(F32)
                d = dif_e[f, HALO + l].astype(F32)
                if side == 0:
                    tile = jnp.where(upper, x[0:8], pltpu.roll(d[0:8], 4, 0))
                else:
                    tile = jnp.where(upper, pltpu.roll(d[LON - 8 :], 4, 0), x[LON - 8 :])
                tiles.append(tile)
            pack[side, l] = jnp.concatenate(tiles, axis=0).astype(BF16)

    def packing():
        for l in range(LEV):
            pack_level(l)

    def wait_fields():
        l_inc.wait()
        l_dif.wait()

    run(0, wait_fields)
    run(0, packing)

    def comm_barrier():
        senders = (
            2
            + 3 * has_low.astype(jnp.int32)
            + 3 * has_high.astype(jnp.int32)
            + (nz - 1)
            + nb
            - (g == hub).astype(jnp.int32)
        )
        pl.semaphore_wait(barrier, senders)

    run(0, comm_barrier)

    def halo_copies(strips, lon_to, lev_pairs, send, recv):
        def copy(k, src, dst, band, lev):
            return pltpu.make_async_remote_copy(
                src_ref=src,
                dst_ref=dst,
                send_sem=send.at[k],
                recv_sem=recv.at[k],
                device_id=(band, lev),
                device_id_type=MESH,
            )

        level, up, down = [], [], []
        sides = (left, right)
        for i, (src, base, dst) in enumerate(lev_pairs):
            up.append(
                copy(6 + i, src.at[:, base + LEV - HALO : base + LEV], dst.at[:, 0:HALO], b, g + 1)
            )
            down.append(
                copy(8 + i, src.at[:, base : base + HALO], dst.at[:, EXT - HALO :], b, g - 1)
            )
        for k in (0, 1):
            level.append(copy(k, strips.at[k], lon_to.at[k, HALO : HALO + LEV], sides[k], g))
            up.append(copy(2 + k, strips.at[k, LEV - 2 :], lon_to.at[k, 1:HALO], sides[k], g + 1))
            down.append(
                copy(4 + k, strips.at[k, 0:2], lon_to.at[k, EXT - HALO : EXT - 1], sides[k], g - 1)
            )
        return level, up, down

    def halo_start(level, up, down):
        for c in level:
            c.start()
        for has, copies in ((has_high, up), (has_low, down)):

            @pl.when(has)
            def _():
                for c in copies:
                    c.start()

    def halo_arrive(level, up, down):
        for c in level:
            c.wait_recv()
        for has, copies in ((has_low, up), (has_high, down)):

            @pl.when(has)
            def _():
                for c in copies:
                    c.wait_recv()

    def halo_sent(level, up, down):
        for c in level:
            c.wait_send()
        for has, copies in ((has_high, up), (has_low, down)):

            @pl.when(has)
            def _():
                for c in copies:
                    c.wait_send()

    halo = halo_copies(
        pack, lon_r, ((inc_hbm, 0, inc_e), (dif_hbm, 0, dif_e)), halo_send, halo_recv
    )

    def comm_halo():
        halo_start(*halo)

    run(1, comm_halo)

    def comm_tabs():
        pltpu.make_async_copy(jac_hbm, tabs.at[core, z], tab_sem.at[1]).start()

        @pl.loop(0, nz)
        def _(other):
            @pl.when(other != z)
            def _():
                pltpu.make_async_remote_copy(
                    src_ref=jac_hbm,
                    dst_ref=tabs.at[core, z],
                    send_sem=tab_sem.at[0],
                    recv_sem=tab_sem.at[1],
                    device_id=(b, 2 * other + core),
                    device_id_type=MESH,
                ).start()

    run(5, comm_tabs)

    def col_row(i):
        return jnp.concatenate([col_v[pl.ds(2 * i, 1)], col_v[pl.ds(2 * i + 1, 1)]], axis=1)

    def lon_low(cols):
        return lax.shift_right_logical(cols, 7) & 15

    def build_hot(i):
        cols = col_row(i)
        want = (lax.shift_right_logical(cols, 11) & 1) * LAT + (cols & (LAT - 1))
        iota = lax.broadcasted_iota(jnp.int32, (2 * LAT, PAIR), 0)
        hot[:, pl.ds(pl.multiple_of(i * PAIR, PAIR), PAIR)] = jnp.where(
            iota == want, 1.0, 0.0
        ).astype(BF16)

    def make_hot():
        pl.loop(0, nb // 2)(build_hot)

    run(0, l_col.wait)
    run(2, make_hot)

    def comm_halo_arrive():
        halo_arrive(*halo)

    run(1, comm_halo_arrive)

    def widen_level(e):
        first = lon_r[0, e].astype(F32)
        last = lon_r[1, e].astype(F32)
        for f in range(FIELDS):
            r = first[8 * f : 8 * f + 8]
            l = last[8 * f : 8 * f + 8]
            ua[f, e, LON:] = jnp.where(upper, r, l)
            dfx[f, e, LON:] = pltpu.roll(jnp.where(upper, l, r), 4, 0)
            ua[f, e, 0:LON] = inc_e[f, e].astype(F32)
            dfx[f, e, 0:LON] = dif_e[f, e].astype(F32)

    def widen():
        pl.loop(0, EXT)(widen_level)

    run(3, widen)

    lane = lax.broadcasted_iota(jnp.int32, (ROWS, LAT), 1)

    def lap(ref, f, e):
        c = ref[f, e]
        total = ref[f, e - 1] + ref[f, e + 1]
        total = total + (pltpu.roll(c, 1, 0) + pltpu.roll(c, ROWS - 1, 0))
        total = total + jnp.where(lane == 0, 0.0, pltpu.roll(c, 1, 1))
        total = total + jnp.where(lane == LAT - 1, 0.0, pltpu.roll(c, LAT - 1, 1))
        return total - 6.0 * c

    def forward(src, dst, step):
        def body(e):
            for f in range(FIELDS):
                dst[f, e] = src[f, e] + dfx[f, e] * lap(src, f, e)

        pl.loop(step, EXT - step)(body)

    def last_step(l):
        for f in range(FIELDS):
            e = l + HALO
            field = (uc[f, e] + dfx[f, e] * lap(uc, f, e))[0:LON]
            st[pl.ds(pl.multiple_of((f * LEV + l) * LON, LON), LON)] = (
                sig_v[f, l].astype(F32) * field
            )

    def diffuse():
        forward(ua, ub, 1)
        forward(ub, uc, 2)
        pl.loop(0, LEV)(last_step)

    run(0, l_sig.wait)
    run(3, diffuse)

    def lay_out():
        for lon in range(LON):
            parts = [st[pl.ds(f * LEV * LON + lon, LEV, stride=LON)] for f in range(FIELDS)]
            s_mat[
                (lon % 16) * WIDTH : (lon % 16 + 1) * WIDTH,
                (lon // 16) * LAT : (lon // 16 + 1) * LAT,
            ] = jnp.concatenate(parts, axis=0).astype(BF16)

    run(4, lay_out)

    def pick(i):
        cols = col_row(i)
        low = lon_low(cols)
        chunk = hot[:, pl.ds(pl.multiple_of(i * PAIR, PAIR), PAIR)]
        rows = dot(s_mat[...], chunk, ((1,), (0,)))
        total = jnp.zeros((WIDTH, PAIR), F32)
        for k in range(16):
            total = jnp.where(low == k, rows[k * WIDTH : (k + 1) * WIDTH], total)
        total = total.astype(BF16)
        for half in range(2):
            prof[2 * i + half] = total[:, half * CAP : (half + 1) * CAP]

    def comm_profile(owner):
        here = jnp.logical_and(owner == b, g == hub)
        slot = arr.at[b % per, core, z]

        @pl.when(here)
        def _():
            pltpu.make_async_copy(prof.at[owner], slot, x_sem.at[1]).start()
            pltpu.make_async_copy(prof.at[owner], junk.at[0], x_sem.at[0]).start()

        @pl.when(jnp.logical_not(here))
        def _():
            pltpu.make_async_remote_copy(
                src_ref=prof.at[owner],
                dst_ref=slot,
                send_sem=x_sem.at[0],
                recv_sem=x_sem.at[1],
                device_id=(owner, hub),
                device_id_type=MESH,
            ).start()

    def gather():
        @pl.loop(0, nb // 2)
        def _(i):
            run(4, functools.partial(pick, i))
            for half in range(2):
                run(5, functools.partial(comm_profile, 2 * i + half))

    run(4, gather)

    share = pltpu.make_async_remote_copy(
        src_ref=tabs.at[core],
        dst_ref=tabs.at[core],
        send_sem=tab_sem.at[2],
        recv_sem=tab_sem.at[3],
        device_id=(b, g + 1 - 2 * core),
        device_id_type=MESH,
    )

    def comm_share():
        pltpu.make_async_copy(tabs.at[0], tabs.at[0], tab_sem.at[1]).wait()
        share.start()

    run(5, comm_share)

    def wait_rest():
        l_inn.wait()
        l_tab.wait()
        l_rinv.wait()
        l_cnt.wait()

    run(0, wait_rest)

    def spread_inn(i):
        at = pl.ds(pl.multiple_of(i * 8, 8), 8)
        inn_f[pl.ds(pl.multiple_of(i * 8 * inn_rows, 8 * inn_rows), 8 * inn_rows)] = (
            inn_v[at].astype(F32).reshape(8 * inn_rows, CAP)
        )

    def innovations():
        pl.loop(0, channels // 8)(spread_inn)
        row = lax.rem(per * g, inn_rows)
        for j in range(per):
            for i in range(channels // 8):
                inn_s[8 * i : 8 * i + 8, j * CAP : (j + 1) * CAP] = inn_f[
                    pl.ds(i * 8 * inn_rows + row + j, 8, stride=inn_rows)
                ]
        for i in range(channels // 128):
            line = rinv_v[:, i * 128 : (i + 1) * 128]
            rcol[i * 128 : (i + 1) * 128] = jnp.broadcast_to(line, (128, 128)).T

    run(6, innovations)

    def comm_tabs_arrive():
        pltpu.make_async_copy(tabs.at[0], tabs.at[0], tab_sem.at[3]).wait()

    run(5, comm_tabs_arrive)

    def table(t):
        return tabs[:, :, t].reshape(ng * WIDTH, channels)

    def turn_tables():
        for t in range(NTAB):
            tabs_t[t] = table(t).T

    run(6, turn_tables)

    def comm_arr():
        pltpu.make_async_copy(arr, arr, x_sem.at[1]).wait()

    run(5, comm_arr)

    def observe():
        profiles = jnp.concatenate(
            [arr[j].reshape(ng * WIDTH, CAP) for j in range(per)], axis=1
        )
        kinds = jnp.concatenate([tab_v[pl.ds(per * g + j, 1)] for j in range(per)], axis=1)
        slot_id = lax.broadcasted_iota(jnp.int32, (1, CAP), 1)
        valid = jnp.concatenate(
            [(slot_id < cnt_s[0, per * g + j]).astype(jnp.int32) for j in range(per)], axis=1
        )
        evolved = jnp.zeros((channels, per * CAP), F32)
        for t in range(NTAB):
            evolved = jnp.where(kinds == t, dot(tabs_t[t], profiles, ((1,), (0,))), evolved)
        scale = jnp.concatenate([rcol[...]] * per, axis=1)
        resid = jnp.where(valid > 0, scale * (evolved - inn_s[...]), 0.0)
        total = jnp.zeros((ng * WIDTH, per * CAP), F32)
        for t in range(NTAB):
            masked = jnp.where(kinds == t, resid, 0.0).astype(BF16)
            total = total + dot(table(t), masked, ((1,), (0,)))
        for j in range(per):
            back[j] = (
                total[:, j * CAP : (j + 1) * CAP].astype(BF16).reshape(2, nz, WIDTH, CAP)
            )

    run(7, observe)

    def comm_back():
        @pl.loop(0, per * ng)
        def _(index):
            j, lev = index // ng, index % ng
            band = per * g + j
            here = jnp.logical_and(band == b, lev == g)
            src = back.at[j, lev % 2, lev // 2]

            @pl.when(here)
            def _():
                pltpu.make_async_copy(src, home.at[b], x_sem.at[3]).start()
                pltpu.make_async_copy(src, junk.at[1], x_sem.at[2]).start()

            @pl.when(jnp.logical_not(here))
            def _():
                pltpu.make_async_remote_copy(
                    src_ref=src,
                    dst_ref=home.at[b],
                    send_sem=x_sem.at[2],
                    recv_sem=x_sem.at[3],
                    device_id=(band, lev),
                    device_id_type=MESH,
                ).start()

        pltpu.make_async_copy(home, home, x_sem.at[3]).wait()

    run(8, comm_back)

    def spread_home(i):
        low = lon_low(col_row(i))
        block = jnp.concatenate([home[2 * i], home[2 * i + 1]], axis=1).astype(F32)
        at = pl.ds(pl.multiple_of(i * PAIR, PAIR), PAIR)
        for k in range(16):
            a_mat[k * WIDTH : (k + 1) * WIDTH, at] = jnp.where(low == k, block, 0.0).astype(BF16)

    def spread():
        pl.loop(0, nb // 2)(spread_home)

    run(9, spread)

    def scatter():
        sums = dot(a_mat[...], hot[...], ((1,), (1,)))
        for k in range(2):
            adj[k * 256 : (k + 1) * 256] = sums[:, k * LAT : (k + 1) * LAT]

    run(9, scatter)

    def weigh():
        for l in range(LEV):
            firsts, lasts = [], []
            for f in range(FIELDS):
                for i in range(LON // 8):
                    cells = adj[pl.ds(i * 8 * WIDTH + f * LEV + l, 8, stride=WIDTH)]
                    w = sig_v[f, l, 8 * i : 8 * i + 8].astype(F32) * cells
                    ua[f, HALO + l, 8 * i : 8 * i + 8] = w
                    if i == 0:
                        firsts.append(w)
                    if i == LON // 8 - 1:
                        lasts.append(w)
            pack_w[0, l] = jnp.concatenate(firsts, axis=0).astype(BF16)
            pack_w[1, l] = jnp.concatenate(lasts, axis=0).astype(BF16)
            for f in range(FIELDS):
                w_e[f, HALO + l] = ua[f, HALO + l, 0:LON].astype(BF16)

    run(9, weigh)

    halo2 = halo_copies(pack_w, lon_w, ((w_e, HALO, w_e),), w_send, w_recv)

    def comm_halo2():
        halo_start(*halo2)
        halo_arrive(*halo2)

    run(10, comm_halo2)

    def widen_w():
        for e in range(EXT):
            first = lon_w[0, e].astype(F32)
            last = lon_w[1, e].astype(F32)
            for f in range(FIELDS):
                ua[f, e, LON:] = jnp.where(
                    upper, first[8 * f : 8 * f + 8], last[8 * f : 8 * f + 8]
                )
                if e < HALO or e >= HALO + LEV:
                    ua[f, e, 0:LON] = w_e[f, e].astype(F32)

    run(11, widen_w)

    def scale_level(e):
        for f in range(FIELDS):
            ub[f, e] = dfx[f, e] * ua[f, e]

    def backward(src, dst, step):
        def body(e):
            for f in range(FIELDS):
                w = ua[f, e] + lap(src, f, e)
                ua[f, e] = w
                dst[f, e] = dfx[f, e] * w

        pl.loop(step, EXT - step)(body)

    def finish(l):
        for f in range(FIELDS):
            e = l + HALO
            w = (ua[f, e] + lap(ub, f, e))[0:LON]
            out_v[f, l] = inc_e[f, e].astype(F32) + w

    def diffuse_back():
        pl.loop(0, EXT)(scale_level)
        backward(ub, uc, 1)
        backward(uc, ub, 2)
        pl.loop(0, LEV)(finish)

    run(11, diffuse_back)
    result = pltpu.make_async_copy(out_v, out_hbm, load_sem.at[8])
    result.start()

    def comm_gone():
        if nz > 1:
            gone = tabs.at[0, 0 : nz - 1]
            pltpu.make_async_copy(gone, gone, tab_sem.at[0]).wait()
        share.wait_send()
        pltpu.make_async_copy(prof, prof, x_sem.at[0]).wait()

    def comm_home_gone():
        pltpu.make_async_copy(back, back, x_sem.at[2]).wait()

    def comm_halo_gone():
        halo_sent(*halo)

    def comm_halo2_gone():
        halo_sent(*halo2)

    run(1, comm_halo_gone)
    run(5, comm_gone)
    run(8, comm_home_gone)
    run(10, comm_halo2_gone)
    result.wait()


def body(
    nb,
    ng,
    increment,
    diffusivity,
    sigma,
    jacobian,
    rinv,
    innovation,
    obs_column,
    obs_table,
    obs_count,
):
    channels = jacobian.shape[1]
    tables = jnp.transpose(jacobian, (0, 2, 3, 1)).reshape(NTAB, WIDTH, channels)
    per, nz = nb // ng, ng // 2
    hbm = pl.BlockSpec(memory_space=pltpu.HBM)
    dma = pltpu.SemaphoreType.DMA
    extended = pltpu.VMEM((FIELDS, EXT, LON, LAT), BF16)
    wide = pltpu.VMEM((FIELDS, EXT, ROWS, LAT), F32)
    return pl.pallas_call(
        functools.partial(kernel, nb, ng),
        out_shape=jax.ShapeDtypeStruct((FIELDS, LEV, LON, LAT), F32),
        in_specs=[hbm] * 9,
        out_specs=hbm,
        scratch_shapes=[
            pltpu.VMEM((FIELDS, LEV, LON, LAT), F32),
            extended,
            extended,
            pltpu.VMEM((FIELDS, LEV, LON, LAT), BF16),
            pltpu.VMEM((1, channels), F32),
            pltpu.SMEM((1, nb), jnp.int32),
            pltpu.VMEM((nb, CAP), jnp.int32),
            pltpu.VMEM((nb, CAP), jnp.int32),
            pltpu.VMEM((channels, min(16, nb), CAP), BF16),
            pltpu.VMEM((channels * min(16, nb), CAP), F32),
            pltpu.VMEM((channels, per * CAP), F32),
            pltpu.VMEM((2, LEV, 16, LAT), BF16),
            pltpu.VMEM((2, EXT, 16, LAT), BF16),
            pltpu.VMEM((2, LEV, 16, LAT), BF16),
            pltpu.VMEM((2, EXT, 16, LAT), BF16),
            extended,
            wide,
            wide,
            wide,
            wide,
            pltpu.VMEM((WIDTH * LON, LAT), F32),
            pltpu.VMEM((16 * WIDTH, 2 * LAT), BF16),
            pltpu.VMEM((2 * LAT, nb * CAP), BF16),
            pltpu.VMEM((16 * WIDTH, nb * CAP), BF16),
            pltpu.VMEM((WIDTH * LON, LAT), F32),
            pltpu.VMEM((nb, WIDTH, CAP), BF16),
            pltpu.VMEM((per, 2, nz, WIDTH, CAP), BF16),
            pltpu.VMEM((2, WIDTH, CAP), BF16),
            pltpu.VMEM((2, nz, NTAB, WIDTH, channels), BF16),
            pltpu.VMEM((NTAB, channels, ng * WIDTH), BF16),
            pltpu.VMEM((channels, CAP), F32),
            pltpu.VMEM((per, 2, nz, WIDTH, CAP), BF16),
            pltpu.VMEM((nb, WIDTH, CAP), BF16),
            dma((9,)),
            dma((10,)),
            dma((10,)),
            dma((10,)),
            dma((10,)),
            dma((4,)),
            dma((4,)),
        ],
        compiler_params=pltpu.CompilerParams(
            collective_id=0, has_side_effects=True, vmem_limit_bytes=60 * 1024 * 1024
        ),
    )(
        increment,
        diffusivity,
        sigma,
        tables,
        rinv.reshape(1, channels),
        innovation,
        obs_column,
        obs_table,
        obs_count,
    )


def solution(mesh):
    in_specs = (
        P(None, "lev", "band", None),
        P(None, "lev", "band", None),
        P(None, "lev", "band", None),
        P(None, None, None, "lev"),
        P(),
        P("band", None, None, None),
        P("band", None, None),
        P("band", None, None),
        P("band", None),
    )
    out_specs = P(None, "lev", "band", None)
    run = functools.partial(body, mesh.shape["band"], mesh.shape["lev"])
    return jax.shard_map(run, mesh=mesh, in_specs=in_specs, out_specs=out_specs, check_vma=False)
```

time: 67 us -> 59.9 us (0.89)
  local copies, waits for them, and re-layouts: 8.53 us -> 1.67 us
    unnamed x19 -> x1, local copies, waits for them, and re-layouts: 8.53 us -> 1.67 us
where the time goes in v2:
time: 59.9 us; the launch traced here: 59.7 us
  Pallas kernels  58 us (97%)
  local copies, waits for them, and re-layouts  1.67 us (3%)
    pallas_call x1, Pallas kernels, body(): pl.pallas_call(functools.partial(kernel, nb, ng), out_shape=jax.ShapeDtyp...  58 us
    unnamed x1, local copies, waits for them, and re-layouts  1.67 us

profile of v2, /device:TPU:1, one launch (start us, length us, event | category | flops | bytes accessed | tf_op | source)
XLA Modules:
  0.0 59.7 jit_solution(562733826103201388)
XLA Ops:
  0.0 58.0 %shard_map.91 = f32[2,8,32,128]{3,2,1,0:T(8,128)} custom-call(bf16[2,8,32,128]{3,2,1,0:T(8,128)(2,1)} %inc_hbm.1, bf16[2,8,32,128]{3,2,1,0:T(8,128)(2,1)} %dif_hbm.1, bf16[2,8,32,128]{3,2,1,0:T(8,128)(2,1)} %sig_hbm.1, bf16[4,16,256]{2,1,0:T(8,128)(2,1)} %bitcast.4, f32[1,256]{1,0:T(1,128)} %bitcast.5, bf16[1,256,32,128]{3,2,1,0:T(8,128)(2,1)} %inn_hbm.1, ...), custom_call_target="tpu_custom_call" | custom-call | tf_op jit(solution)/shard_map/pallas_call | solution.py:673
  58.1 1.7 %copy.11 = f32[2,8,32,128]{3,2,1,0:T(8,128)} copy(f32[2,8,32,128]{3,2,1,0:T(8,128)} %shard_map.91) | data formatting | bytes 524288

commit v3 on v2

--- a/solution.py
+++ b/solution.py
@@ -57,6 +57,7 @@
     inn_v,
     inn_f,
     inn_s,
+    inn_r,
     pack,
     lon_r,
     pack_w,
@@ -86,13 +87,14 @@
     w_recv,
     tab_sem,
     x_sem,
+    swap_sem,
 ):
     b, g = lax.axis_index("band"), lax.axis_index("lev")
-    per = nb // ng
     nz = ng // 2
     z, core = g // 2, g % 2
     left, right = lax.rem(b + nb - 1, nb), lax.rem(b + 1, nb)
-    hub = b // per
+    mate = lax.rem(g + ng - lax.rem(b // 2, ng), ng)
+    own_mate = mate == b // 2
     has_low, has_high = g > 0, g < ng - 1
     channels = inn_v.shape[0]
     inn_rows = inn_v.shape[1]
@@ -109,7 +111,7 @@
             inn_hbm.at[
                 0,
                 :,
-                pl.ds(pl.multiple_of((per * g) // inn_rows * inn_rows, inn_rows), inn_rows),
+                pl.ds(pl.multiple_of((2 * mate) // inn_rows * inn_rows, inn_rows), inn_rows),
             ],
             inn_v,
             load_sem.at[7],
@@ -129,30 +131,25 @@
 
             @pl.when(has)
             def _():
-                for side in (left, b, right):
+                for side in (left, right):
                     greet(side, lev)
 
-        @pl.loop(0, nz)
-        def _(other):
-            @pl.when(other != z)
-            def _():
-                greet(b, 2 * other + core)
-
-        @pl.loop(0, per * ng)
-        def _(index):
-            band, lev = per * g + index // ng, index % ng
-
-            @pl.when(jnp.logical_or(band != b, lev != g))
-            def _():
-                greet(band, lev)
-
-    run(0, comm_greet)
+        @pl.loop(1, ng)
+        def _(i):
+            greet(b, lax.rem(g + i, ng))
+
+        for j in range(2):
+
+            @pl.when(2 * mate + j != b)
+            def _():
+                greet(2 * mate + j, g)
 
     def start_loads():
         for load in loads:
             load.start()
 
     run(0, start_loads)
+    run(0, comm_greet)
 
     zeros = jnp.zeros((FIELDS, HALO, LON, LAT), BF16)
     zeros_lon = jnp.zeros((2, HALO, 16, LAT), BF16)
@@ -204,11 +201,11 @@
     def comm_barrier():
         senders = (
             2
-            + 3 * has_low.astype(jnp.int32)
-            + 3 * has_high.astype(jnp.int32)
-            + (nz - 1)
-            + nb
-            - (g == hub).astype(jnp.int32)
+            + 2 * has_low.astype(jnp.int32)
+            + 2 * has_high.astype(jnp.int32)
+            + (ng - 1)
+            + 2
+            - own_mate.astype(jnp.int32)
         )
         pl.semaphore_wait(barrier, senders)
 
@@ -299,6 +296,71 @@
 
     run(5, comm_tabs)
 
+    def wait_observations():
+        l_inn.wait()
+        l_tab.wait()
+        l_rinv.wait()
+        l_cnt.wait()
+
+    run(0, wait_observations)
+
+    def spread_inn(i):
+        at = pl.ds(pl.multiple_of(i * 8, 8), 8)
+        inn_f[pl.ds(pl.multiple_of(i * 8 * inn_rows, 8 * inn_rows), 8 * inn_rows)] = (
+            inn_v[at].astype(F32).reshape(8 * inn_rows, CAP)
+        )
+
+    def innovations():
+        pl.loop(0, channels // 8)(spread_inn)
+        row = lax.rem(2 * mate, inn_rows)
+        slot_id = lax.broadcasted_iota(jnp.int32, (16, CAP), 1)
+        for j in range(2):
+            for i in range(channels // 16):
+                halves = [
+                    inn_f[pl.ds((2 * i + k) * 8 * inn_rows + row + j, 8, stride=inn_rows)]
+                    for k in range(2)
+                ]
+                inn_s[j, 16 * i : 16 * i + 16] = jnp.concatenate(halves, axis=0).astype(BF16)
+            kinds = jnp.broadcast_to(tab_v[pl.ds(2 * mate + j, 1)], (16, CAP))
+            kinds = jnp.where(slot_id < cnt_s[0, 2 * mate + j], kinds, -1)
+            inn_s[j, channels:] = kinds.astype(F32).astype(BF16)
+
+    run(6, innovations)
+
+    def swap_copy(j):
+        return pltpu.make_async_remote_copy(
+            src_ref=inn_s.at[j],
+            dst_ref=inn_r.at[b % 2],
+            send_sem=swap_sem.at[j],
+            recv_sem=swap_sem.at[2],
+            device_id=(2 * mate + j, g),
+            device_id_type=MESH,
+        )
+
+    def comm_swap():
+        for j in range(2):
+            here = 2 * mate + j == b
+
+            @pl.when(here)
+            def _():
+                pltpu.make_async_copy(inn_s.at[j], inn_r.at[b % 2], swap_sem.at[2]).start()
+
+            @pl.when(jnp.logical_not(here))
+            def _():
+                swap_copy(j).start()
+
+    def comm_swap_gone():
+        for j in range(2):
+
+            @pl.when(2 * mate + j != b)
+            def _():
+                swap_copy(j).wait_send()
+
+    def comm_swap_arrive():
+        pltpu.make_async_copy(inn_r, inn_r, swap_sem.at[2]).wait()
+
+    run(5, comm_swap)
+
     def col_row(i):
         return jnp.concatenate([col_v[pl.ds(2 * i, 1)], col_v[pl.ds(2 * i + 1, 1)]], axis=1)
 
@@ -391,36 +453,34 @@
         total = jnp.zeros((WIDTH, PAIR), F32)
         for k in range(16):
             total = jnp.where(low == k, rows[k * WIDTH : (k + 1) * WIDTH], total)
-        total = total.astype(BF16)
-        for half in range(2):
-            prof[2 * i + half] = total[:, half * CAP : (half + 1) * CAP]
-
-    def comm_profile(owner):
-        here = jnp.logical_and(owner == b, g == hub)
-        slot = arr.at[b % per, core, z]
-
-        @pl.when(here)
-        def _():
-            pltpu.make_async_copy(prof.at[owner], slot, x_sem.at[1]).start()
-            pltpu.make_async_copy(prof.at[owner], junk.at[0], x_sem.at[0]).start()
-
-        @pl.when(jnp.logical_not(here))
-        def _():
-            pltpu.make_async_remote_copy(
-                src_ref=prof.at[owner],
-                dst_ref=slot,
-                send_sem=x_sem.at[0],
-                recv_sem=x_sem.at[1],
-                device_id=(owner, hub),
-                device_id_type=MESH,
-            ).start()
+        prof[i] = total.astype(BF16)
+
+    def comm_profile(i, lev):
+        pltpu.make_async_remote_copy(
+            src_ref=prof.at[i],
+            dst_ref=arr.at[core, z],
+            send_sem=x_sem.at[0],
+            recv_sem=x_sem.at[1],
+            device_id=(b, lev),
+            device_id_type=MESH,
+        ).start()
+
+    def comm_profile_own(i):
+        pltpu.make_async_copy(prof.at[i], arr.at[core, z], x_sem.at[1]).start()
+        pltpu.make_async_copy(prof.at[i], junk.at[0], x_sem.at[0]).start()
+
+    hops = sorted(range(nz), key=lambda d: -min(d, nz - d))
+    order = [(d, c) for d in hops for c in (0, 1) if (d, c) != (0, 0)] + [(0, 0)]
 
     def gather():
-        @pl.loop(0, nb // 2)
-        def _(i):
+        for d, c in order:
+            lev = 2 * lax.rem(z + d, nz) + (core + c) % 2
+            i = lax.rem(lev + ng - lax.rem(b // 2, ng), ng)
             run(4, functools.partial(pick, i))
-            for half in range(2):
-                run(5, functools.partial(comm_profile, 2 * i + half))
+            if (d, c) == (0, 0):
+                run(5, functools.partial(comm_profile_own, i))
+            else:
+                run(5, functools.partial(comm_profile, i, lev))
 
     run(4, gather)
 
@@ -439,33 +499,12 @@
 
     run(5, comm_share)
 
-    def wait_rest():
-        l_inn.wait()
-        l_tab.wait()
-        l_rinv.wait()
-        l_cnt.wait()
-
-    run(0, wait_rest)
-
-    def spread_inn(i):
-        at = pl.ds(pl.multiple_of(i * 8, 8), 8)
-        inn_f[pl.ds(pl.multiple_of(i * 8 * inn_rows, 8 * inn_rows), 8 * inn_rows)] = (
-            inn_v[at].astype(F32).reshape(8 * inn_rows, CAP)
-        )
-
-    def innovations():
-        pl.loop(0, channels // 8)(spread_inn)
-        row = lax.rem(per * g, inn_rows)
-        for j in range(per):
-            for i in range(channels // 8):
-                inn_s[8 * i : 8 * i + 8, j * CAP : (j + 1) * CAP] = inn_f[
-                    pl.ds(i * 8 * inn_rows + row + j, 8, stride=inn_rows)
-                ]
+    def turn_rinv():
         for i in range(channels // 128):
             line = rinv_v[:, i * 128 : (i + 1) * 128]
             rcol[i * 128 : (i + 1) * 128] = jnp.broadcast_to(line, (128, 128)).T
 
-    run(6, innovations)
+    run(6, turn_rinv)
 
     def comm_tabs_arrive():
         pltpu.make_async_copy(tabs.at[0], tabs.at[0], tab_sem.at[3]).wait()
@@ -487,61 +526,48 @@
     run(5, comm_arr)
 
     def observe():
-        profiles = jnp.concatenate(
-            [arr[j].reshape(ng * WIDTH, CAP) for j in range(per)], axis=1
+        profiles = arr[...].reshape(ng * WIDTH, PAIR)
+        kinds = jnp.concatenate(
+            [inn_r[j, channels:].astype(F32)[0:1] for j in range(2)], axis=1
         )
-        kinds = jnp.concatenate([tab_v[pl.ds(per * g + j, 1)] for j in range(per)], axis=1)
-        slot_id = lax.broadcasted_iota(jnp.int32, (1, CAP), 1)
-        valid = jnp.concatenate(
-            [(slot_id < cnt_s[0, per * g + j]).astype(jnp.int32) for j in range(per)], axis=1
-        )
-        evolved = jnp.zeros((channels, per * CAP), F32)
+        seen = jnp.concatenate([inn_r[j, 0:channels].astype(F32) for j in range(2)], axis=1)
+        evolved = jnp.zeros((channels, PAIR), F32)
         for t in range(NTAB):
             evolved = jnp.where(kinds == t, dot(tabs_t[t], profiles, ((1,), (0,))), evolved)
-        scale = jnp.concatenate([rcol[...]] * per, axis=1)
-        resid = jnp.where(valid > 0, scale * (evolved - inn_s[...]), 0.0)
-        total = jnp.zeros((ng * WIDTH, per * CAP), F32)
+        scale = jnp.concatenate([rcol[...]] * 2, axis=1)
+        resid = scale * (evolved - seen)
+        total = jnp.zeros((ng * WIDTH, PAIR), F32)
         for t in range(NTAB):
             masked = jnp.where(kinds == t, resid, 0.0).astype(BF16)
             total = total + dot(table(t), masked, ((1,), (0,)))
-        for j in range(per):
-            back[j] = (
-                total[:, j * CAP : (j + 1) * CAP].astype(BF16).reshape(2, nz, WIDTH, CAP)
-            )
-
+        back[...] = total.astype(BF16).reshape(2, nz, WIDTH, PAIR)
+
+    run(5, comm_swap_arrive)
     run(7, observe)
 
     def comm_back():
-        @pl.loop(0, per * ng)
-        def _(index):
-            j, lev = index // ng, index % ng
-            band = per * g + j
-            here = jnp.logical_and(band == b, lev == g)
-            src = back.at[j, lev % 2, lev // 2]
-
-            @pl.when(here)
-            def _():
-                pltpu.make_async_copy(src, home.at[b], x_sem.at[3]).start()
+        for d, c in order:
+            oz, oc = lax.rem(z + d, nz), (core + c) % 2
+            src = back.at[oc, oz]
+            if (d, c) == (0, 0):
+                pltpu.make_async_copy(src, home.at[mate], x_sem.at[3]).start()
                 pltpu.make_async_copy(src, junk.at[1], x_sem.at[2]).start()
-
-            @pl.when(jnp.logical_not(here))
-            def _():
+            else:
                 pltpu.make_async_remote_copy(
                     src_ref=src,
-                    dst_ref=home.at[b],
+                    dst_ref=home.at[mate],
                     send_sem=x_sem.at[2],
                     recv_sem=x_sem.at[3],
-                    device_id=(band, lev),
+                    device_id=(b, 2 * oz + oc),
                     device_id_type=MESH,
                 ).start()
-
         pltpu.make_async_copy(home, home, x_sem.at[3]).wait()
 
     run(8, comm_back)
 
     def spread_home(i):
         low = lon_low(col_row(i))
-        block = jnp.concatenate([home[2 * i], home[2 * i + 1]], axis=1).astype(F32)
+        block = home[i].astype(F32)
         at = pl.ds(pl.multiple_of(i * PAIR, PAIR), PAIR)
         for k in range(16):
             a_mat[k * WIDTH : (k + 1) * WIDTH, at] = jnp.where(low == k, block, 0.0).astype(BF16)
@@ -644,6 +670,7 @@
         halo_sent(*halo2)
 
     run(1, comm_halo_gone)
+    run(5, comm_swap_gone)
     run(5, comm_gone)
     run(8, comm_home_gone)
     run(10, comm_halo2_gone)
@@ -665,7 +692,7 @@
 ):
     channels = jacobian.shape[1]
     tables = jnp.transpose(jacobian, (0, 2, 3, 1)).reshape(NTAB, WIDTH, channels)
-    per, nz = nb // ng, ng // 2
+    nz = ng // 2
     hbm = pl.BlockSpec(memory_space=pltpu.HBM)
     dma = pltpu.SemaphoreType.DMA
     extended = pltpu.VMEM((FIELDS, EXT, LON, LAT), BF16)
@@ -686,7 +713,8 @@
             pltpu.VMEM((nb, CAP), jnp.int32),
             pltpu.VMEM((channels, min(16, nb), CAP), BF16),
             pltpu.VMEM((channels * min(16, nb), CAP), F32),
-            pltpu.VMEM((channels, per * CAP), F32),
+            pltpu.VMEM((2, channels + 16, CAP), BF16),
+            pltpu.VMEM((2, channels + 16, CAP), BF16),
             pltpu.VMEM((2, LEV, 16, LAT), BF16),
             pltpu.VMEM((2, EXT, 16, LAT), BF16),
             pltpu.VMEM((2, LEV, 16, LAT), BF16),
@@ -701,14 +729,14 @@
             pltpu.VMEM((2 * LAT, nb * CAP), BF16),
             pltpu.VMEM((16 * WIDTH, nb * CAP), BF16),
             pltpu.VMEM((WIDTH * LON, LAT), F32),
-            pltpu.VMEM((nb, WIDTH, CAP), BF16),
-            pltpu.VMEM((per, 2, nz, WIDTH, CAP), BF16),
-            pltpu.VMEM((2, WIDTH, CAP), BF16),
+            pltpu.VMEM((ng, WIDTH, PAIR), BF16),
+            pltpu.VMEM((2, nz, WIDTH, PAIR), BF16),
+            pltpu.VMEM((2, WIDTH, PAIR), BF16),
             pltpu.VMEM((2, nz, NTAB, WIDTH, channels), BF16),
             pltpu.VMEM((NTAB, channels, ng * WIDTH), BF16),
             pltpu.VMEM((channels, CAP), F32),
-            pltpu.VMEM((per, 2, nz, WIDTH, CAP), BF16),
-            pltpu.VMEM((nb, WIDTH, CAP), BF16),
+            pltpu.VMEM((2, nz, WIDTH, PAIR), BF16),
+            pltpu.VMEM((ng, WIDTH, PAIR), BF16),
             dma((9,)),
             dma((10,)),
             dma((10,)),
@@ -716,6 +744,7 @@
             dma((10,)),
             dma((4,)),
             dma((4,)),
+            dma((3,)),
         ],
         compiler_params=pltpu.CompilerParams(
             collective_id=0, has_side_effects=True, vmem_limit_bytes=60 * 1024 * 1024

time: 59.9 us -> 50.9 us (0.85)
  Pallas kernels: 58 us -> 49.1 us
    pallas_call x1, Pallas kernels: 58 us -> 49.1 us  [body(): pl.pallas_call(functools.partial(kernel, nb, ng), out_shape=jax.ShapeDtyp...]
where the time goes in v3:
time: 50.9 us; the launch traced here: 50.7 us
  Pallas kernels  49.1 us (96%)
  local copies, waits for them, and re-layouts  1.67 us (3%)
    pallas_call x1, Pallas kernels, body(): pl.pallas_call(functools.partial(kernel, nb, ng), out_shape=jax.ShapeDtyp...  49.1 us
    unnamed x1, local copies, waits for them, and re-layouts  1.67 us

profile of v3, /device:TPU:1, one launch (start us, length us, event | category | flops | bytes accessed | tf_op | source)
XLA Modules:
  0.0 50.7 jit_solution(4542615102646977497)
XLA Ops:
  0.0 49.1 %shard_map.91 = f32[2,8,32,128]{3,2,1,0:T(8,128)} custom-call(bf16[2,8,32,128]{3,2,1,0:T(8,128)(2,1)} %inc_hbm.1, bf16[2,8,32,128]{3,2,1,0:T(8,128)(2,1)} %dif_hbm.1, bf16[2,8,32,128]{3,2,1,0:T(8,128)(2,1)} %sig_hbm.1, bf16[4,16,256]{2,1,0:T(8,128)(2,1)} %bitcast.4, f32[1,256]{1,0:T(1,128)} %bitcast.5, bf16[1,256,32,128]{3,2,1,0:T(8,128)(2,1)} %inn_hbm.1, ...), custom_call_target="tpu_custom_call" | custom-call | tf_op jit(solution)/shard_map/pallas_call | solution.py:700
  49.1 1.7 %copy.11 = f32[2,8,32,128]{3,2,1,0:T(8,128)} copy(f32[2,8,32,128]{3,2,1,0:T(8,128)} %shard_map.91) | data formatting | bytes 524288

commit v4 on v3

--- a/solution.py
+++ b/solution.py
@@ -27,6 +27,22 @@
 
 def dot(a, b, dims):
     return lax.dot_general(a, b, (dims, ((), ())), preferred_element_type=F32)
+
+
+def gap(lev, ng):
+    rank = ng - 1 - lev
+    if ng != 16:
+        return 0, rank, 1, ng
+    long, short = rank // 4, rank % 4
+    turn = lambda k: k + (k >= 2).astype(jnp.int32) - 2 * (k >= 3).astype(jnp.int32)
+    return turn(short), turn(long), 4, 4
+
+
+def pair_on(pair, lev, ng, sign):
+    dx, dy, nx, ny = gap(lev, ng)
+    x = lax.rem(pair // ny + nx + sign * dx, nx)
+    y = lax.rem(pair % ny + ny + sign * dy, ny)
+    return x * ny + y
 
 
 def run(step, work):
@@ -93,11 +109,15 @@
     nz = ng // 2
     z, core = g // 2, g % 2
     left, right = lax.rem(b + nb - 1, nb), lax.rem(b + 1, nb)
-    mate = lax.rem(g + ng - lax.rem(b // 2, ng), ng)
-    own_mate = mate == b // 2
+    to_pair = pair_on(b // 2, g, ng, 1)
+    from_pair = pair_on(b // 2, g, ng, -1)
+    own_pair = to_pair == b // 2
     has_low, has_high = g > 0, g < ng - 1
     channels = inn_v.shape[0]
     inn_rows = inn_v.shape[1]
+
+    hops = sorted(range(nz), key=lambda d: -min(d, nz - d))
+    order = [(d, c) for d in hops for c in (0, 1) if (d, c) != (0, 0)] + [(0, 0)]
 
     loads = [
         pltpu.make_async_copy(inc_hbm, inc_e.at[:, HALO : HALO + LEV], load_sem.at[0]),
@@ -111,7 +131,7 @@
             inn_hbm.at[
                 0,
                 :,
-                pl.ds(pl.multiple_of((2 * mate) // inn_rows * inn_rows, inn_rows), inn_rows),
+                pl.ds(pl.multiple_of((2 * to_pair) // inn_rows * inn_rows, inn_rows), inn_rows),
             ],
             inn_v,
             load_sem.at[7],
@@ -125,8 +145,14 @@
         pl.semaphore_signal(barrier, inc=1, device_id=(band, lev), device_id_type=MESH)
 
     def comm_greet():
-        for side in (left, right):
-            greet(side, g)
+        for d, c in order[:-1]:
+            greet(b, 2 * lax.rem(z + d, nz) + (core + c) % 2)
+        for j in range(2):
+
+            @pl.when(2 * from_pair + j != b)
+            def _():
+                greet(2 * from_pair + j, g)
+
         for has, lev in ((has_low, g - 1), (has_high, g + 1)):
 
             @pl.when(has)
@@ -134,22 +160,15 @@
                 for side in (left, right):
                     greet(side, lev)
 
-        @pl.loop(1, ng)
-        def _(i):
-            greet(b, lax.rem(g + i, ng))
-
-        for j in range(2):
-
-            @pl.when(2 * mate + j != b)
-            def _():
-                greet(2 * mate + j, g)
+        for side in (left, right):
+            greet(side, g)
 
     def start_loads():
         for load in loads:
             load.start()
 
+    run(0, comm_greet)
     run(0, start_loads)
-    run(0, comm_greet)
 
     zeros = jnp.zeros((FIELDS, HALO, LON, LAT), BF16)
     zeros_lon = jnp.zeros((2, HALO, 16, LAT), BF16)
@@ -163,11 +182,12 @@
                 dif_e[:, at] = zeros
                 w_e[:, at] = zeros
                 lon_r[:, at] = zeros_lon
-                lon_w[:, at] = zeros_lon
+                lon_w[:, 0 if edge == 0 else LEV // 2 + 1] = zeros_lon[:, 0]
 
         for e in (0, EXT - 1):
             lon_r[:, e] = zeros_lon[:, 0]
-            lon_w[:, e] = zeros_lon[:, 0]
+            for f in range(FIELDS):
+                ua[f, e, LON:] = jnp.zeros((8, LAT), F32)
 
     run(0, clear)
 
@@ -205,7 +225,7 @@
             + 2 * has_high.astype(jnp.int32)
             + (ng - 1)
             + 2
-            - own_mate.astype(jnp.int32)
+            - own_pair.astype(jnp.int32)
         )
         pl.semaphore_wait(barrier, senders)
 
@@ -224,29 +244,43 @@
 
         level, up, down = [], [], []
         sides = (left, right)
-        for i, (src, base, dst) in enumerate(lev_pairs):
+        count = strips.shape[1]
+        edge = 2 * count // LEV
+        base = (lon_to.shape[1] - count) // 2
+        for k in (0, 1):
+            level.append(copy(k, strips.at[k], lon_to.at[k, base : base + count], sides[k], g))
             up.append(
-                copy(6 + i, src.at[:, base + LEV - HALO : base + LEV], dst.at[:, 0:HALO], b, g + 1)
+                copy(2 + k, strips.at[k, count - edge :], lon_to.at[k, base - edge : base], sides[k], g + 1)
             )
             down.append(
-                copy(8 + i, src.at[:, base : base + HALO], dst.at[:, EXT - HALO :], b, g - 1)
+                copy(
+                    4 + k,
+                    strips.at[k, 0:edge],
+                    lon_to.at[k, base + count : base + count + edge],
+                    sides[k],
+                    g - 1,
+                )
             )
-        for k in (0, 1):
-            level.append(copy(k, strips.at[k], lon_to.at[k, HALO : HALO + LEV], sides[k], g))
-            up.append(copy(2 + k, strips.at[k, LEV - 2 :], lon_to.at[k, 1:HALO], sides[k], g + 1))
+        for i, (src, first, dst) in enumerate(lev_pairs):
+            up.append(
+                copy(6 + i, src.at[:, first + LEV - HALO : first + LEV], dst.at[:, 0:HALO], b, g + 1)
+            )
             down.append(
-                copy(4 + k, strips.at[k, 0:2], lon_to.at[k, EXT - HALO : EXT - 1], sides[k], g - 1)
+                copy(8 + i, src.at[:, first : first + HALO], dst.at[:, EXT - HALO :], b, g - 1)
             )
         return level, up, down
 
     def halo_start(level, up, down):
-        for c in level:
-            c.start()
-        for has, copies in ((has_high, up), (has_low, down)):
-
-            @pl.when(has)
-            def _():
-                for c in copies:
+        for part in (slice(0, 2), slice(2, None)):
+            for has, copies in ((has_high, up), (has_low, down)):
+
+                @pl.when(has)
+                def _():
+                    for c in copies[part]:
+                        c.start()
+
+            if part.start == 0:
+                for c in level:
                     c.start()
 
     def halo_arrive(level, up, down):
@@ -281,18 +315,15 @@
     def comm_tabs():
         pltpu.make_async_copy(jac_hbm, tabs.at[core, z], tab_sem.at[1]).start()
 
-        @pl.loop(0, nz)
-        def _(other):
-            @pl.when(other != z)
-            def _():
-                pltpu.make_async_remote_copy(
-                    src_ref=jac_hbm,
-                    dst_ref=tabs.at[core, z],
-                    send_sem=tab_sem.at[0],
-                    recv_sem=tab_sem.at[1],
-                    device_id=(b, 2 * other + core),
-                    device_id_type=MESH,
-                ).start()
+        for d in hops[:-1]:
+            pltpu.make_async_remote_copy(
+                src_ref=jac_hbm,
+                dst_ref=tabs.at[core, z],
+                send_sem=tab_sem.at[0],
+                recv_sem=tab_sem.at[1],
+                device_id=(b, 2 * lax.rem(z + d, nz) + core),
+                device_id_type=MESH,
+            ).start()
 
     run(5, comm_tabs)
 
@@ -312,7 +343,7 @@
 
     def innovations():
         pl.loop(0, channels // 8)(spread_inn)
-        row = lax.rem(2 * mate, inn_rows)
+        row = lax.rem(2 * to_pair, inn_rows)
         slot_id = lax.broadcasted_iota(jnp.int32, (16, CAP), 1)
         for j in range(2):
             for i in range(channels // 16):
@@ -321,8 +352,8 @@
                     for k in range(2)
                 ]
                 inn_s[j, 16 * i : 16 * i + 16] = jnp.concatenate(halves, axis=0).astype(BF16)
-            kinds = jnp.broadcast_to(tab_v[pl.ds(2 * mate + j, 1)], (16, CAP))
-            kinds = jnp.where(slot_id < cnt_s[0, 2 * mate + j], kinds, -1)
+            kinds = jnp.broadcast_to(tab_v[pl.ds(2 * to_pair + j, 1)], (16, CAP))
+            kinds = jnp.where(slot_id < cnt_s[0, 2 * to_pair + j], kinds, -1)
             inn_s[j, channels:] = kinds.astype(F32).astype(BF16)
 
     run(6, innovations)
@@ -333,13 +364,13 @@
             dst_ref=inn_r.at[b % 2],
             send_sem=swap_sem.at[j],
             recv_sem=swap_sem.at[2],
-            device_id=(2 * mate + j, g),
+            device_id=(2 * to_pair + j, g),
             device_id_type=MESH,
         )
 
     def comm_swap():
         for j in range(2):
-            here = 2 * mate + j == b
+            here = 2 * to_pair + j == b
 
             @pl.when(here)
             def _():
@@ -352,7 +383,7 @@
     def comm_swap_gone():
         for j in range(2):
 
-            @pl.when(2 * mate + j != b)
+            @pl.when(2 * to_pair + j != b)
             def _():
                 swap_copy(j).wait_send()
 
@@ -398,7 +429,8 @@
             dfx[f, e, 0:LON] = dif_e[f, e].astype(F32)
 
     def widen():
-        pl.loop(0, EXT)(widen_level)
+        for e in range(EXT):
+            widen_level(e)
 
     run(3, widen)
 
@@ -413,24 +445,23 @@
         return total - 6.0 * c
 
     def forward(src, dst, step):
-        def body(e):
+        for e in range(step, EXT - step):
             for f in range(FIELDS):
                 dst[f, e] = src[f, e] + dfx[f, e] * lap(src, f, e)
-
-        pl.loop(step, EXT - step)(body)
 
     def last_step(l):
         for f in range(FIELDS):
             e = l + HALO
             field = (uc[f, e] + dfx[f, e] * lap(uc, f, e))[0:LON]
-            st[pl.ds(pl.multiple_of((f * LEV + l) * LON, LON), LON)] = (
+            st[(f * LEV + l) * LON : (f * LEV + l + 1) * LON] = (
                 sig_v[f, l].astype(F32) * field
             )
 
     def diffuse():
         forward(ua, ub, 1)
         forward(ub, uc, 2)
-        pl.loop(0, LEV)(last_step)
+        for l in range(LEV):
+            last_step(l)
 
     run(0, l_sig.wait)
     run(3, diffuse)
@@ -469,13 +500,10 @@
         pltpu.make_async_copy(prof.at[i], arr.at[core, z], x_sem.at[1]).start()
         pltpu.make_async_copy(prof.at[i], junk.at[0], x_sem.at[0]).start()
 
-    hops = sorted(range(nz), key=lambda d: -min(d, nz - d))
-    order = [(d, c) for d in hops for c in (0, 1) if (d, c) != (0, 0)] + [(0, 0)]
-
     def gather():
         for d, c in order:
             lev = 2 * lax.rem(z + d, nz) + (core + c) % 2
-            i = lax.rem(lev + ng - lax.rem(b // 2, ng), ng)
+            i = pair_on(b // 2, lev, ng, -1)
             run(4, functools.partial(pick, i))
             if (d, c) == (0, 0):
                 run(5, functools.partial(comm_profile_own, i))
@@ -550,12 +578,12 @@
             oz, oc = lax.rem(z + d, nz), (core + c) % 2
             src = back.at[oc, oz]
             if (d, c) == (0, 0):
-                pltpu.make_async_copy(src, home.at[mate], x_sem.at[3]).start()
+                pltpu.make_async_copy(src, home.at[from_pair], x_sem.at[3]).start()
                 pltpu.make_async_copy(src, junk.at[1], x_sem.at[2]).start()
             else:
                 pltpu.make_async_remote_copy(
                     src_ref=src,
-                    dst_ref=home.at[mate],
+                    dst_ref=home.at[from_pair],
                     send_sem=x_sem.at[2],
                     recv_sem=x_sem.at[3],
                     device_id=(b, 2 * oz + oc),
@@ -585,21 +613,24 @@
     run(9, scatter)
 
     def weigh():
-        for l in range(LEV):
+        for l in range(0, LEV, 2):
             firsts, lasts = [], []
-            for f in range(FIELDS):
-                for i in range(LON // 8):
-                    cells = adj[pl.ds(i * 8 * WIDTH + f * LEV + l, 8, stride=WIDTH)]
-                    w = sig_v[f, l, 8 * i : 8 * i + 8].astype(F32) * cells
-                    ua[f, HALO + l, 8 * i : 8 * i + 8] = w
-                    if i == 0:
-                        firsts.append(w)
-                    if i == LON // 8 - 1:
-                        lasts.append(w)
-            pack_w[0, l] = jnp.concatenate(firsts, axis=0).astype(BF16)
-            pack_w[1, l] = jnp.concatenate(lasts, axis=0).astype(BF16)
-            for f in range(FIELDS):
-                w_e[f, HALO + l] = ua[f, HALO + l, 0:LON].astype(BF16)
+            for k in (l, l + 1):
+                tiles = []
+                for f in range(FIELDS):
+                    for i in range(LON // 8):
+                        cells = adj[pl.ds(i * 8 * WIDTH + f * LEV + k, 8, stride=WIDTH)]
+                        w = sig_v[f, k, 8 * i : 8 * i + 8].astype(F32) * cells
+                        ua[f, HALO + k, 8 * i : 8 * i + 8] = w
+                        tiles.append(w)
+                firsts.append(jnp.where(upper, tiles[0], pltpu.roll(tiles[LON // 8], 4, 0)))
+                lasts.append(jnp.where(upper, pltpu.roll(tiles[LON // 8 - 1], 4, 0), tiles[-1]))
+            pack_w[0, l // 2] = jnp.concatenate(firsts, axis=0).astype(BF16)
+            pack_w[1, l // 2] = jnp.concatenate(lasts, axis=0).astype(BF16)
+            for k in (l, l + 1):
+                if k < HALO or k >= LEV - HALO:
+                    for f in range(FIELDS):
+                        w_e[f, HALO + k] = ua[f, HALO + k, 0:LON].astype(BF16)
 
     run(9, weigh)
 
@@ -612,13 +643,15 @@
     run(10, comm_halo2)
 
     def widen_w():
-        for e in range(EXT):
-            first = lon_w[0, e].astype(F32)
-            last = lon_w[1, e].astype(F32)
-            for f in range(FIELDS):
-                ua[f, e, LON:] = jnp.where(
-                    upper, first[8 * f : 8 * f + 8], last[8 * f : 8 * f + 8]
-                )
+        for i in range(LEV // 2 + 2):
+            for k in (0, 1):
+                e = 1 + 2 * i + k
+                first = lon_w[0, i].astype(F32)[8 * k : 8 * k + 8]
+                last = lon_w[1, i].astype(F32)[8 * k : 8 * k + 8]
+                ua[0, e, LON:] = jnp.where(upper, first, pltpu.roll(last, 4, 0))
+                ua[1, e, LON:] = jnp.where(upper, pltpu.roll(first, 4, 0), last)
+        for f in range(FIELDS):
+            for e in range(EXT):
                 if e < HALO or e >= HALO + LEV:
                     ua[f, e, 0:LON] = w_e[f, e].astype(F32)
 
@@ -629,13 +662,11 @@
             ub[f, e] = dfx[f, e] * ua[f, e]
 
     def backward(src, dst, step):
-        def body(e):
+        for e in range(step, EXT - step):
             for f in range(FIELDS):
                 w = ua[f, e] + lap(src, f, e)
                 ua[f, e] = w
                 dst[f, e] = dfx[f, e] * w
-
-        pl.loop(step, EXT - step)(body)
 
     def finish(l):
         for f in range(FIELDS):
@@ -644,20 +675,24 @@
             out_v[f, l] = inc_e[f, e].astype(F32) + w
 
     def diffuse_back():
-        pl.loop(0, EXT)(scale_level)
+        for e in range(EXT):
+            scale_level(e)
         backward(ub, uc, 1)
         backward(uc, ub, 2)
-        pl.loop(0, LEV)(finish)
+        for l in range(LEV):
+            finish(l)
 
     run(11, diffuse_back)
     result = pltpu.make_async_copy(out_v, out_hbm, load_sem.at[8])
     result.start()
 
-    def comm_gone():
+    def comm_tabs_gone():
         if nz > 1:
             gone = tabs.at[0, 0 : nz - 1]
             pltpu.make_async_copy(gone, gone, tab_sem.at[0]).wait()
         share.wait_send()
+
+    def comm_profiles_gone():
         pltpu.make_async_copy(prof, prof, x_sem.at[0]).wait()
 
     def comm_home_gone():
@@ -671,7 +706,8 @@
 
     run(1, comm_halo_gone)
     run(5, comm_swap_gone)
-    run(5, comm_gone)
+    run(5, comm_tabs_gone)
+    run(5, comm_profiles_gone)
     run(8, comm_home_gone)
     run(10, comm_halo2_gone)
     result.wait()
@@ -717,8 +753,8 @@
             pltpu.VMEM((2, channels + 16, CAP), BF16),
             pltpu.VMEM((2, LEV, 16, LAT), BF16),
             pltpu.VMEM((2, EXT, 16, LAT), BF16),
-            pltpu.VMEM((2, LEV, 16, LAT), BF16),
-            pltpu.VMEM((2, EXT, 16, LAT), BF16),
+            pltpu.VMEM((2, LEV // 2, 16, LAT), BF16),
+            pltpu.VMEM((2, LEV // 2 + 2, 16, LAT), BF16),
             extended,
             wide,
             wide,

time: 50.9 us -> 44.1 us (0.87)
  Pallas kernels: 49.1 us -> 42.3 us
    pallas_call x1, Pallas kernels: 49.1 us -> 42.3 us  [body(): pl.pallas_call(functools.partial(kernel, nb, ng), out_shape=jax.ShapeDtyp...]
where the time goes in v4:
time: 44.1 us; the launch traced here: 44 us
  Pallas kernels  42.3 us (96%)
  local copies, waits for them, and re-layouts  1.67 us (4%)
    pallas_call x1, Pallas kernels, body(): pl.pallas_call(functools.partial(kernel, nb, ng), out_shape=jax.ShapeDtyp...  42.3 us
    unnamed x1, local copies, waits for them, and re-layouts  1.67 us

profile of v4, /device:TPU:1, one launch (start us, length us, event | category | flops | bytes accessed | tf_op | source)
XLA Modules:
  0.0 44.0 jit_solution(16977659800331837483)
XLA Ops:
  0.0 42.3 %shard_map.91 = f32[2,8,32,128]{3,2,1,0:T(8,128)} custom-call(bf16[2,8,32,128]{3,2,1,0:T(8,128)(2,1)} %inc_hbm.1, bf16[2,8,32,128]{3,2,1,0:T(8,128)(2,1)} %dif_hbm.1, bf16[2,8,32,128]{3,2,1,0:T(8,128)(2,1)} %sig_hbm.1, bf16[4,16,256]{2,1,0:T(8,128)(2,1)} %bitcast.4, f32[1,256]{1,0:T(1,128)} %bitcast.5, bf16[1,256,32,128]{3,2,1,0:T(8,128)(2,1)} %inn_hbm.1, ...), custom_call_target="tpu_custom_call" | custom-call | tf_op jit(solution)/shard_map/pallas_call | solution.py:736
  42.3 1.7 %copy.11 = f32[2,8,32,128]{3,2,1,0:T(8,128)} copy(f32[2,8,32,128]{3,2,1,0:T(8,128)} %shard_map.91) | data formatting | bytes 524288

commit v5 on v4

--- a/solution.py
+++ b/solution.py
@@ -61,7 +61,6 @@
     col_hbm,
     tab_hbm,
     cnt_hbm,
-    out_hbm,
     out_v,
     inc_e,
     dif_e,
@@ -69,6 +68,7 @@
     rinv_v,
     cnt_s,
     col_v,
+    cols,
     tab_v,
     inn_v,
     inn_f,
@@ -86,6 +86,7 @@
     st,
     s_mat,
     hot,
+    hot_t,
     a_mat,
     adj,
     prof,
@@ -119,6 +120,14 @@
     hops = sorted(range(nz), key=lambda d: -min(d, nz - d))
     order = [(d, c) for d in hops for c in (0, 1) if (d, c) != (0, 0)] + [(0, 0)]
 
+    place = {at: k for k, at in enumerate(order)}
+    groups = {}
+    for k, (d, c) in enumerate(order):
+        groups.setdefault(max(1, min(d, nz - d)), []).append(k)
+    groups = [(dist, min(ks), max(ks) + 1) for dist, ks in sorted(groups.items())]
+    levs = [2 * lax.rem(z + d, nz) + (core + c) % 2 for d, c in order]
+    owners = [pair_on(b // 2, lev, ng, -1) for lev in levs]
+
     loads = [
         pltpu.make_async_copy(inc_hbm, inc_e.at[:, HALO : HALO + LEV], load_sem.at[0]),
         pltpu.make_async_copy(dif_hbm, dif_e.at[:, HALO : HALO + LEV], load_sem.at[1]),
@@ -392,24 +401,28 @@
 
     run(5, comm_swap)
 
-    def col_row(i):
-        return jnp.concatenate([col_v[pl.ds(2 * i, 1)], col_v[pl.ds(2 * i + 1, 1)]], axis=1)
-
-    def lon_low(cols):
-        return lax.shift_right_logical(cols, 7) & 15
-
-    def build_hot(i):
-        cols = col_row(i)
-        want = (lax.shift_right_logical(cols, 11) & 1) * LAT + (cols & (LAT - 1))
+    def sort_cols():
+        for k, i in enumerate(owners):
+            cols[k : k + 1] = jnp.concatenate(
+                [col_v[pl.ds(2 * i, 1)], col_v[pl.ds(2 * i + 1, 1)]], axis=1
+            )
+
+    def lon_low(line):
+        return lax.shift_right_logical(line, 7) & 15
+
+    def build_hot(k):
+        line = cols[pl.ds(k, 1)]
+        want = (lax.shift_right_logical(line, 11) & 1) * LAT + (line & (LAT - 1))
         iota = lax.broadcasted_iota(jnp.int32, (2 * LAT, PAIR), 0)
-        hot[:, pl.ds(pl.multiple_of(i * PAIR, PAIR), PAIR)] = jnp.where(
+        hot[:, pl.ds(pl.multiple_of(k * PAIR, PAIR), PAIR)] = jnp.where(
             iota == want, 1.0, 0.0
         ).astype(BF16)
 
     def make_hot():
-        pl.loop(0, nb // 2)(build_hot)
+        pl.loop(0, ng)(build_hot)
 
     run(0, l_col.wait)
+    run(0, sort_cols)
     run(2, make_hot)
 
     def comm_halo_arrive():
@@ -476,39 +489,32 @@
 
     run(4, lay_out)
 
-    def pick(i):
-        cols = col_row(i)
-        low = lon_low(cols)
-        chunk = hot[:, pl.ds(pl.multiple_of(i * PAIR, PAIR), PAIR)]
-        rows = dot(s_mat[...], chunk, ((1,), (0,)))
+    def pick(k):
+        low = lon_low(cols[k : k + 1])
+        rows = dot(s_mat[...], hot[:, k * PAIR : (k + 1) * PAIR], ((1,), (0,)))
         total = jnp.zeros((WIDTH, PAIR), F32)
-        for k in range(16):
-            total = jnp.where(low == k, rows[k * WIDTH : (k + 1) * WIDTH], total)
-        prof[i] = total.astype(BF16)
-
-    def comm_profile(i, lev):
-        pltpu.make_async_remote_copy(
-            src_ref=prof.at[i],
-            dst_ref=arr.at[core, z],
-            send_sem=x_sem.at[0],
-            recv_sem=x_sem.at[1],
-            device_id=(b, lev),
-            device_id_type=MESH,
-        ).start()
-
-    def comm_profile_own(i):
-        pltpu.make_async_copy(prof.at[i], arr.at[core, z], x_sem.at[1]).start()
-        pltpu.make_async_copy(prof.at[i], junk.at[0], x_sem.at[0]).start()
+        for n in range(16):
+            total = jnp.where(low == n, rows[n * WIDTH : (n + 1) * WIDTH], total)
+        prof[k] = total.astype(BF16)
+
+    def comm_profile(k):
+        if order[k] == (0, 0):
+            pltpu.make_async_copy(prof.at[k], arr.at[core, z], x_sem.at[1]).start()
+            pltpu.make_async_copy(prof.at[k], junk.at[0], x_sem.at[0]).start()
+        else:
+            pltpu.make_async_remote_copy(
+                src_ref=prof.at[k],
+                dst_ref=arr.at[core, z],
+                send_sem=x_sem.at[0],
+                recv_sem=x_sem.at[1],
+                device_id=(b, levs[k]),
+                device_id_type=MESH,
+            ).start()
 
     def gather():
-        for d, c in order:
-            lev = 2 * lax.rem(z + d, nz) + (core + c) % 2
-            i = pair_on(b // 2, lev, ng, -1)
-            run(4, functools.partial(pick, i))
-            if (d, c) == (0, 0):
-                run(5, functools.partial(comm_profile_own, i))
-            else:
-                run(5, functools.partial(comm_profile, i, lev))
+        for k in range(ng):
+            run(4, functools.partial(pick, k))
+            run(5, functools.partial(comm_profile, k))
 
     run(4, gather)
 
@@ -547,6 +553,13 @@
             tabs_t[t] = table(t).T
 
     run(6, turn_tables)
+
+    def turn_hot():
+        for k in range(ng):
+            at = slice(k * PAIR, (k + 1) * PAIR)
+            hot_t[at] = hot[:, at].T
+
+    run(6, turn_hot)
 
     def comm_arr():
         pltpu.make_async_copy(arr, arr, x_sem.at[1]).wait()
@@ -574,43 +587,53 @@
     run(7, observe)
 
     def comm_back():
-        for d, c in order:
-            oz, oc = lax.rem(z + d, nz), (core + c) % 2
-            src = back.at[oc, oz]
+        for k, (d, c) in enumerate(order):
+            src = back.at[(core + c) % 2, lax.rem(z + d, nz)]
+            there = place[(nz - d) % nz, c]
+            arrives = x_sem.at[2 + max(1, min(d, nz - d))]
             if (d, c) == (0, 0):
-                pltpu.make_async_copy(src, home.at[from_pair], x_sem.at[3]).start()
+                pltpu.make_async_copy(src, home.at[there], arrives).start()
                 pltpu.make_async_copy(src, junk.at[1], x_sem.at[2]).start()
             else:
                 pltpu.make_async_remote_copy(
                     src_ref=src,
-                    dst_ref=home.at[from_pair],
+                    dst_ref=home.at[there],
                     send_sem=x_sem.at[2],
-                    recv_sem=x_sem.at[3],
-                    device_id=(b, 2 * oz + oc),
+                    recv_sem=arrives,
+                    device_id=(b, levs[k]),
                     device_id_type=MESH,
                 ).start()
-        pltpu.make_async_copy(home, home, x_sem.at[3]).wait()
 
     run(8, comm_back)
 
-    def spread_home(i):
-        low = lon_low(col_row(i))
-        block = home[i].astype(F32)
-        at = pl.ds(pl.multiple_of(i * PAIR, PAIR), PAIR)
-        for k in range(16):
-            a_mat[k * WIDTH : (k + 1) * WIDTH, at] = jnp.where(low == k, block, 0.0).astype(BF16)
-
-    def spread():
-        pl.loop(0, nb // 2)(spread_home)
-
-    run(9, spread)
-
-    def scatter():
-        sums = dot(a_mat[...], hot[...], ((1,), (1,)))
+    def comm_home(dist, lo, hi):
+        part = home.at[lo:hi]
+        pltpu.make_async_copy(part, part, x_sem.at[2 + dist]).wait()
+
+    def spread(lo, hi):
+        for k in range(lo, hi):
+            low = jnp.broadcast_to(lon_low(cols[k : k + 1]).astype(F32), (WIDTH, PAIR)).astype(BF16)
+            block = home[k]
+            for n in range(16):
+                a_mat[n * WIDTH : (n + 1) * WIDTH, k * PAIR : (k + 1) * PAIR] = jnp.where(
+                    low == jnp.asarray(n, BF16), block, jnp.zeros_like(block)
+                )
+
+    def scatter(lo, hi):
+        at = slice(lo * PAIR, hi * PAIR)
+        part = dot(a_mat[:, at], hot_t[at], ((1,), (0,)))
         for k in range(2):
-            adj[k * 256 : (k + 1) * 256] = sums[:, k * LAT : (k + 1) * LAT]
-
-    run(9, scatter)
+            half = part[:, k * LAT : (k + 1) * LAT]
+            rows = slice(k * 16 * WIDTH, (k + 1) * 16 * WIDTH)
+            if lo == groups[0][1]:
+                adj[rows] = half
+            else:
+                adj[rows] += half
+
+    for group in groups:
+        run(8, functools.partial(comm_home, *group))
+        run(9, functools.partial(spread, *group[1:]))
+        run(9, functools.partial(scatter, *group[1:]))
 
     def weigh():
         for l in range(0, LEV, 2):
@@ -683,8 +706,6 @@
             finish(l)
 
     run(11, diffuse_back)
-    result = pltpu.make_async_copy(out_v, out_hbm, load_sem.at[8])
-    result.start()
 
     def comm_tabs_gone():
         if nz > 1:
@@ -710,7 +731,6 @@
     run(5, comm_profiles_gone)
     run(8, comm_home_gone)
     run(10, comm_halo2_gone)
-    result.wait()
 
 
 def body(
@@ -735,17 +755,17 @@
     wide = pltpu.VMEM((FIELDS, EXT, ROWS, LAT), F32)
     return pl.pallas_call(
         functools.partial(kernel, nb, ng),
-        out_shape=jax.ShapeDtypeStruct((FIELDS, LEV, LON, LAT), F32),
+        out_shape=pltpu.VMEM((FIELDS, LEV, LON, LAT), F32),
         in_specs=[hbm] * 9,
-        out_specs=hbm,
+        out_specs=pl.BlockSpec(memory_space=pltpu.VMEM),
         scratch_shapes=[
-            pltpu.VMEM((FIELDS, LEV, LON, LAT), F32),
             extended,
             extended,
             pltpu.VMEM((FIELDS, LEV, LON, LAT), BF16),
             pltpu.VMEM((1, channels), F32),
             pltpu.SMEM((1, nb), jnp.int32),
             pltpu.VMEM((nb, CAP), jnp.int32),
+            pltpu.VMEM((ng, PAIR), jnp.int32),
             pltpu.VMEM((nb, CAP), jnp.int32),
             pltpu.VMEM((channels, min(16, nb), CAP), BF16),
             pltpu.VMEM((channels * min(16, nb), CAP), F32),
@@ -763,6 +783,7 @@
             pltpu.VMEM((WIDTH * LON, LAT), F32),
             pltpu.VMEM((16 * WIDTH, 2 * LAT), BF16),
             pltpu.VMEM((2 * LAT, nb * CAP), BF16),
+            pltpu.VMEM((nb * CAP, 2 * LAT), BF16),
             pltpu.VMEM((16 * WIDTH, nb * CAP), BF16),
             pltpu.VMEM((WIDTH * LON, LAT), F32),
             pltpu.VMEM((ng, WIDTH, PAIR), BF16),
@@ -773,13 +794,13 @@
             pltpu.VMEM((channels, CAP), F32),
             pltpu.VMEM((2, nz, WIDTH, PAIR), BF16),
             pltpu.VMEM((ng, WIDTH, PAIR), BF16),
-            dma((9,)),
+            dma((8,)),
             dma((10,)),
             dma((10,)),
             dma((10,)),
             dma((10,)),
             dma((4,)),
-            dma((4,)),
+            dma((7,)),
             dma((3,)),
         ],
         compiler_params=pltpu.CompilerParams(

time: 44.1 us -> 41.5 us (0.941)
  Pallas kernels: 42.3 us -> 40.7 us
  local copies, waits for them, and re-layouts: 1.67 us -> 0.71 us
    pallas_call x1, Pallas kernels: 42.3 us -> 40.7 us  [body(): pl.pallas_call(functools.partial(kernel, nb, ng), out_shape=pltpu.VMEM((F...]
    unnamed x1, local copies, waits for them, and re-layouts: 1.67 us -> 0.71 us
where the time goes in v5:
time: 41.5 us; the launch traced here: 41.4 us
  Pallas kernels  40.7 us (98%)
  local copies, waits for them, and re-layouts  0.71 us (2%)
    pallas_call x1, Pallas kernels, body(): pl.pallas_call(functools.partial(kernel, nb, ng), out_shape=pltpu.VMEM((F...  40.7 us

profile of v5, /device:TPU:1, one launch (start us, length us, event | category | flops | bytes accessed | tf_op | source)
XLA Modules:
  0.0 41.4 jit_solution(12490281994768949264)
XLA Ops:
  0.0 40.7 %shard_map.91 = f32[2,8,32,128]{3,2,1,0:T(8,128)S(1)} custom-call(bf16[2,8,32,128]{3,2,1,0:T(8,128)(2,1)} %inc_hbm.1, bf16[2,8,32,128]{3,2,1,0:T(8,128)(2,1)} %dif_hbm.1, bf16[2,8,32,128]{3,2,1,0:T(8,128)(2,1)} %sig_hbm.1, bf16[4,16,256]{2,1,0:T(8,128)(2,1)} %bitcast.4, f32[1,256]{1,0:T(1,128)} %bitcast.5, bf16[1,256,32,128]{3,2,1,0:T(8,128)(2,1)} %inn_hbm.1, ...), custom_call_target="tpu_custom_call" | custom-call | tf_op jit(solution)/shard_map/pallas_call | solution.py:756
  40.7 0.7 %copy.11 = f32[2,8,32,128]{3,2,1,0:T(8,128)} copy(f32[2,8,32,128]{3,2,1,0:T(8,128)S(1)} %shard_map.91) | data formatting | bytes 524288

commit v6 on v5

--- a/solution.py
+++ b/solution.py
@@ -172,10 +172,15 @@
         for side in (left, right):
             greet(side, g)
 
+    def start_first():
+        l_inc.start()
+        l_dif.start()
+
     def start_loads():
-        for load in loads:
+        for load in loads[2:]:
             load.start()
 
+    run(0, start_first)
     run(0, comm_greet)
     run(0, start_loads)
 
@@ -313,7 +318,7 @@
                     c.wait_send()
 
     halo = halo_copies(
-        pack, lon_r, ((inc_hbm, 0, inc_e), (dif_hbm, 0, dif_e)), halo_send, halo_recv
+        pack, lon_r, ((inc_e, HALO, inc_e), (dif_e, HALO, dif_e)), halo_send, halo_recv
     )
 
     def comm_halo():
@@ -334,7 +339,6 @@
                 device_id_type=MESH,
             ).start()
 
-    run(5, comm_tabs)
 
     def wait_observations():
         l_inn.wait()
@@ -424,6 +428,7 @@
     run(0, l_col.wait)
     run(0, sort_cols)
     run(2, make_hot)
+    run(5, comm_tabs)
 
     def comm_halo_arrive():
         halo_arrive(*halo)

time: 41.5 us -> 41.3 us (level)
  no operation moved by 1% of the time
where the time goes in v6:
time: 41.3 us; the launch traced here: 41.2 us
  Pallas kernels  40.5 us (98%)
  local copies, waits for them, and re-layouts  0.71 us (2%)
    pallas_call x1, Pallas kernels, body(): pl.pallas_call(functools.partial(kernel, nb, ng), out_shape=pltpu.VMEM((F...  40.5 us

profile of v6, /device:TPU:1, one launch (start us, length us, event | category | flops | bytes accessed | tf_op | source)
XLA Modules:
  0.0 41.2 jit_solution(1713278515813740187)
XLA Ops:
  0.0 40.5 %shard_map.91 = f32[2,8,32,128]{3,2,1,0:T(8,128)S(1)} custom-call(bf16[2,8,32,128]{3,2,1,0:T(8,128)(2,1)} %inc_hbm.1, bf16[2,8,32,128]{3,2,1,0:T(8,128)(2,1)} %dif_hbm.1, bf16[2,8,32,128]{3,2,1,0:T(8,128)(2,1)} %sig_hbm.1, bf16[4,16,256]{2,1,0:T(8,128)(2,1)} %bitcast.4, f32[1,256]{1,0:T(1,128)} %bitcast.5, bf16[1,256,32,128]{3,2,1,0:T(8,128)(2,1)} %inn_hbm.1, ...), custom_call_target="tpu_custom_call" | custom-call | tf_op jit(solution)/shard_map/pallas_call | solution.py:761
  40.5 0.7 %copy.11 = f32[2,8,32,128]{3,2,1,0:T(8,128)} copy(f32[2,8,32,128]{3,2,1,0:T(8,128)S(1)} %shard_map.91) | data formatting | bytes 524288
